TPU v7x, 32 devices: a whole 2x2x4 slice. The times are simulated.
32 devices in a mesh: ctx: 8 (over z, x), exp: 4 (over y, core).
Axes of the slice: x: 2, y: 2, z: 4, core: 2. Of those that a mesh axis runs over, the one named last changes fastest.
Arguments:
- tokens: bfloat16 [2048, 2880], P('ctx', 'exp'), may hold values from -6 to 6
- cotangent: bfloat16 [2048, 2880], P('ctx', 'exp'), may hold values from -4 to 4
- expert_indices: int32 [2048, 4], P('ctx'), may hold values from 0 to 127, all different within a row; in each aligned block of 256 rows (0 to 255, 256 to 511, ...) at most 16 rows name the same one
- routing_weights: float32 [2048, 4], P('ctx'), may hold values from 0.2 to 1
- gate_up_weight_blocks: bfloat16 [8, 2, 2880, 2880], P('ctx', None, 'exp'), may hold values from -6 to 6
- gate_up_block_scales: float32 [8, 2, 2880, 90], P('ctx', None, 'exp'), may hold values from 0.01 to 0.1
- down_weight_blocks: bfloat16 [8, 2880, 2880], P('ctx', 'exp'), may hold values from -6 to 6
- down_block_scales: float32 [8, 2880, 90], P('ctx', 'exp'), may hold values from 0.002 to 0.008
- adapter_down_matrix: bfloat16 [8, 2880, 16], P('ctx', 'exp'), may hold values from -0.109375 to 0.109375
- adapter_up_matrix: bfloat16 [8, 16, 2880], P('ctx', None, 'exp'), may hold values from -1.5 to 1.5
Outputs:
- moe_out: bfloat16 [2048, 2880], P('ctx', 'exp')
- left_gradient: float32 [8, 2880, 16], P('ctx', 'exp')
- right_gradient: float32 [8, 16, 2880], P('ctx', None, 'exp')
Inputs may be any that keep to these rules, and one draw needn't show every extreme that they name: `expert_indices`: each row names 4 different experts. Within the 256 rows of one index of ctx no expert is named more than 16 times, a bound that some block reaches.
All inputs are finite; a program needn't handle non-finite values.
Results may differ from a plain program's by a relative error of at most 0.018.
Values may be sent and summed in bfloat16 or wider, within the bound.
A program may use at most 64 MiB of HBM per device.

v0:
```python
import jax
import jax.numpy as jnp
from jax import lax
from jax.sharding import PartitionSpec as P

CAP = 16


ADAPTER_SCALE = 0.5
GLU_ALPHA = 1.702
CLAMP_LIMIT = 7.0


def slot_table(expert_indices, flight, capacity):
    flat_ids = expert_indices.reshape(-1)
    onehot = (flat_ids[:, None] == jnp.arange(flight, dtype=jnp.int32)[None, :]).astype(jnp.int32)
    before = jnp.cumsum(onehot, axis=0) - onehot
    position = jnp.sum(before * onehot, axis=1)
    is_live = jnp.sum(onehot, axis=1) > 0
    target = jnp.where(is_live, flat_ids * capacity + position, -1)
    return target.reshape(expert_indices.shape)


def slot_sources(target, slot_count):
    flat_target = target.reshape(-1)
    matches = flat_target[None, :] == jnp.arange(slot_count, dtype=jnp.int32)[:, None]
    pair_index = jnp.arange(flat_target.shape[0], dtype=jnp.int32)
    chosen = jnp.sum(jnp.where(matches, pair_index[None, :], 0), axis=1)
    filled = jnp.any(matches, axis=1)
    return (chosen, filled)


def dispatch_rows(tokens, cotangent, routing_weights, chosen, filled, choices):
    token_of = chosen // choices
    weight_of = jnp.where(filled, routing_weights.reshape(-1)[chosen], 0.0)
    row_data = jnp.where(filled[:, None], tokens[token_of], jnp.zeros((), tokens.dtype))
    gradient_rows = (weight_of[:, None] * cotangent[token_of].astype(jnp.float32)).astype(
        jnp.bfloat16
    )
    return (row_data, gradient_rows)


def dequant_gate_up(blocks, scales):
    pair, hidden, width = blocks.shape
    shaped = blocks.astype(jnp.float32).reshape(pair, hidden, width // 32, 32)
    return (shaped * scales[:, :, :, None]).reshape(pair, hidden, width).astype(jnp.bfloat16)


def dequant_down(blocks, scales):
    hidden, width = blocks.shape
    shaped = blocks.astype(jnp.float32).reshape(hidden, width // 32, 32)
    return (shaped * scales[:, :, None]).reshape(hidden, width).astype(jnp.bfloat16)


def on_device(
    tokens,
    cotangent,
    expert_indices,
    routing_weights,
    gate_up_weight_blocks,
    gate_up_block_scales,
    down_weight_blocks,
    down_block_scales,
    adapter_down_matrix,
    adapter_up_matrix,
):
    flight = lax.axis_size("ctx")
    choices = expert_indices.shape[1]
    slot_count = flight * CAP
    target = slot_table(expert_indices, flight, CAP)
    chosen, filled = slot_sources(target, slot_count)
    w_joined = dequant_gate_up(gate_up_weight_blocks[0], gate_up_block_scales[0])
    w_down = dequant_down(down_weight_blocks[0], down_block_scales[0])
    adapter_left = adapter_down_matrix[0]
    adapter_right = adapter_up_matrix[0]
    whole_rows = lax.all_gather(tokens, "exp", axis=1, tiled=True)
    row_data, gradient_rows = dispatch_rows(
        whole_rows, cotangent, routing_weights, chosen, filled, choices
    )
    got_rows, got_grads = (
        lax.all_to_all(row_data, "ctx", split_axis=0, concat_axis=0, tiled=True),
        lax.all_to_all(gradient_rows, "ctx", split_axis=0, concat_axis=0, tiled=True),
    )
    projected = jnp.einsum("sn,cfn->csf", got_rows, w_joined, preferred_element_type=jnp.float32)
    gate_cut = jnp.minimum(projected[0], CLAMP_LIMIT)
    up_cut = jnp.clip(projected[1], -CLAMP_LIMIT, CLAMP_LIMIT)
    activated = ((up_cut + 1.0) * gate_cut * jax.nn.sigmoid(GLU_ALPHA * gate_cut)).astype(
        jnp.bfloat16
    )
    low_term = jnp.dot(activated, adapter_left, preferred_element_type=jnp.float32)
    back_term = lax.dot_general(
        got_grads, adapter_right, (((1,), (1,)), ((), ())), preferred_element_type=jnp.float32
    )
    low_sum, backward_sum = (
        lax.psum(low_term.astype(jnp.bfloat16), "exp").astype(jnp.float32),
        lax.psum(back_term.astype(jnp.bfloat16), "exp").astype(jnp.float32),
    )
    reduced_rank = low_sum.astype(jnp.bfloat16)
    backward_rank = (ADAPTER_SCALE * backward_sum).astype(jnp.bfloat16)
    base_columns = lax.psum_scatter(
        lax.dot_general(
            w_down, activated, (((0,), (1,)), ((), ())), preferred_element_type=jnp.float32
        ).astype(jnp.bfloat16),
        "exp",
        scatter_dimension=0,
        tiled=True,
    ).astype(jnp.float32)
    adapter_columns = lax.dot_general(
        adapter_right, reduced_rank, (((0,), (1,)), ((), ())), preferred_element_type=jnp.float32
    )
    output_columns = (base_columns + ADAPTER_SCALE * adapter_columns).astype(jnp.bfloat16)
    returned = lax.all_to_all(output_columns, "ctx", split_axis=1, concat_axis=1, tiled=True)
    safe_index = jnp.maximum(target, 0).reshape(-1)
    picked = (
        returned[:, safe_index]
        .astype(jnp.float32)
        .reshape(returned.shape[0], target.shape[0], choices)
    )
    scaled = jnp.where(target >= 0, routing_weights, 0.0)
    moe_out = jnp.sum(picked * scaled[None], axis=2).T.astype(jnp.bfloat16)
    right_gradient = ADAPTER_SCALE * lax.dot_general(
        reduced_rank, got_grads, (((0,), (0,)), ((), ())), preferred_element_type=jnp.float32
    )
    left_gradient = lax.dot_general(
        activated, backward_rank, (((0,), (0,)), ((), ())), preferred_element_type=jnp.float32
    )
    return (moe_out, left_gradient[None], right_gradient[None])


def solution(mesh):
    placed = (
        P("ctx", "exp"),
        P("ctx", "exp"),
        P("ctx", None),
        P("ctx", None),
        P("ctx", None, "exp", None),
        P("ctx", None, "exp", None),
        P("ctx", "exp", None),
        P("ctx", "exp", None),
        P("ctx", "exp", None),
        P("ctx", None, "exp"),
    )
    return jax.shard_map(
        on_device,
        mesh=mesh,
        in_specs=placed,
        out_specs=(P("ctx", "exp"), P("ctx", "exp", None), P("ctx", None, "exp")),
        check_vma=False,
    )
```

profile of v0, /device:TPU:0, one launch (start us, length us, event | category | flops | bytes accessed | tf_op | source)
XLA Modules:
  0.0 129.9 jit_solution(2218853050721028475)
XLA Ops:
  7.2 0.7 all-gather.2.cloned.1.call-update
  7.9 0.8 copy.73
  9.0 11.9 %copy.71 = bf16[1,2,720,2880]{2,3,1,0:T(8,128)(2,1)} copy(bf16[1,2,720,2880]{3,2,1,0:T(8,128)(2,1)} %param.14) | data formatting | bytes 16588800 | tf_op args[4]
  20.9 2.3 %reduce-window.6 = s32[8,8,128]{2,1,0:T(8,128)S(1)} reduce-window(s32[8,8,128]{2,1,0:T(8,128)S(1)} %fusion.17, s32[]{:T(128)} %constant.18.clone.1), window={size=1x1x128 pad=0_0x0_0x127_0}, to_apply=%region_1.2 | reduce-window | flops 1040384 | bytes 65540 | tf_op jit(solution)/shard_map/reduce-window
  24.5 1.0 gather_fusion.2
  25.5 6.5 %copy.70 = bf16[1,720,2880]{1,2,0:T(8,128)(2,1)} copy(bf16[1,720,2880]{2,1,0:T(8,128)(2,1)} %param.16) | data formatting | bytes 8294400 | tf_op args[6]
  32.1 1.8 %copy.75 = bf16[256,2880]{1,0:T(8,128)(2,1)S(1)} copy(bf16[256,2880]{0,1:T(8,128)(2,1)} %all-gather.2.cloned.1.call-done) | data formatting | bytes 2949120 | tf_op jit(solution)/shard_map/all_gather | solution.py:76
  34.0 1.1 gather_fusion
  35.0 1.1 broadcast_select_fusion
  36.1 7.3 %all-to-all-start = ((bf16[8,16,2880]{2,1,0:T(8,128)(2,1)}), bf16[8,16,2880]{2,1,0:T(8,128)(2,1)S(1)}, u32[]{:S(2)}, u32[]{:S(2)}) async-start(bf16[8,16,2880]{2,1,0:T(8,128)(2,1)} %broadcast_select_fusion), calls=%async_computation | async-start | bytes 1507328 | tf_op jit(solution)/shard_map/all_to_all | solution.py:81
  43.6 5.8 %fusion.1 = bf16[720,90,32]{0,2,1:T(8,128)(2,1)} fusion(bf16[720,90,32]{0,2,1:T(8,128)(2,1)} %bitcast.90, f32[720,90]{0,1:T(8,128)S(1)} %bitcast.96), kind=kLoop, calls=%fused_computation.7 | loop fusion | flops 6220800 | bytes 8553600 | tf_op jit(solution)/shard_map/convert_element_type | solution.py:52
  49.4 10.4 %fusion = bf16[2,720,90,32]{1,3,2,0:T(8,128)(2,1)} fusion(bf16[2,720,90,32]{1,3,2,0:T(8,128)(2,1)} %bitcast.88, f32[2,720,90]{1,2,0:T(8,128)S(1)} %copy.72), kind=kLoop, calls=%fused_computation.5 | loop fusion | flops 12441600 | bytes 17107200 | tf_op jit(solution)/shard_map/convert_element_type | solution.py:46
  59.8 3.2 %all-to-all-done = bf16[8,16,2880]{2,1,0:T(8,128)(2,1)S(1)} async-done(((bf16[8,16,2880]{2,1,0:T(8,128)(2,1)}), bf16[8,16,2880]{2,1,0:T(8,128)(2,1)S(1)}, u32[]{:S(2)}, u32[]{:S(2)}) %all-to-all-start) | async-done | bytes 737312 | tf_op jit(solution)/shard_map/all_to_all | solution.py:81
  62.9 6.4 %convolution_bitcast_fusion = f32[2,128,720]{1,2,0:T(8,128)S(1)} fusion(bf16[2,720,2880]{1,2,0:T(8,128)(2,1)} %bitcast.91, bf16[128,2880,1]{1,0,2:T(8,128)(2,1)S(1)} %bitcast.98), kind=kOutput, calls=%fused_computation.11 | convolution fusion | flops 1061683200 | bytes 9768960 | tf_op jit(solution)/shard_map/sn,cfn->csf/dot_general | solution.py:84
  69.5 2.2 %convolution_convert_fusion = bf16[2880,128]{1,0:T(8,128)(2,1)} fusion(bf16[720,2880]{0,1:T(8,128)(2,1)S(1)} %bitcast.89, bf16[1,128,720]{1,2,0:T(8,128)(2,1)S(1)} %fusion.11), kind=kOutput, calls=%fused_computation.8 | convolution fusion | flops 531210240 | bytes 5068800 | tf_op jit(solution)/shard_map/dot_general | solution.py:101
  72.0 0.9 gather_fusion.3
  72.8 0.8 fusion.7
  73.6 3.6 %all-to-all-start.2 = ((bf16[8,16,720]{2,1,0:T(8,128)(2,1)}), bf16[8,16,720]{2,1,0:T(8,128)(2,1)S(1)}, u32[]{:S(2)}, u32[]{:S(2)}) async-start(bf16[8,16,720]{2,1,0:T(8,128)(2,1)} %fusion.7), calls=%async_computation.3 | async-start | bytes 393216 | tf_op jit(solution)/shard_map/all_to_all | solution.py:82
  78.0 7.3 %all-to-all-done.2 = bf16[8,16,720]{2,1,0:T(8,128)(2,1)S(1)} async-done(((bf16[8,16,720]{2,1,0:T(8,128)(2,1)}), bf16[8,16,720]{2,1,0:T(8,128)(2,1)S(1)}, u32[]{:S(2)}, u32[]{:S(2)}) %all-to-all-start.2) | async-done | bytes 184352 | tf_op jit(solution)/shard_map/all_to_all | solution.py:82
  85.6 6.3 %all-reduce = (bf16[128,16]{0,1:T(8,128)(2,1)S(1)}, bf16[128,16]{0,1:T(8,128)(2,1)S(1)}) all-reduce(bf16[128,16]{0,1:T(8,128)(2,1)S(1)} %convolution_convert_fusion.1, bf16[128,16]{0,1:T(8,128)(2,1)S(1)} %convolution_convert_fusion.2), channel_id=1, replica_groups=mesh['ctx'=8,'exp'=4] {'exp'}, use_global_device_ids=true, to_apply=%region_7.8 | all-reduce | flops 4096 | bytes 16384 | tf_op jit(solution)/shard_map/psum | solution.py:95
  92.0 2.1 %reduce-scatter.2.cloned.1.call-done = bf16[720,128]{1,0:T(8,128)(2,1)} async-done(((bf16[2880,128]{1,0:T(8,128)(2,1)}), bf16[720,128]{1,0:T(8,128)(2,1)}) %reduce-scatter.2.cloned.1.call-update) | async-done | bytes 184336 | tf_op jit(solution)/shard_map/reduce_scatter | solution.py:100
  94.1 1.2 fusion.4
  95.3 0.8 copy.78
  96.1 5.3 %all-to-all-start.1 = ((bf16[720,8,16]{0,2,1:T(8,128)(2,1)}), bf16[720,8,16]{0,2,1:T(8,128)(2,1)S(1)}, u32[]{:S(2)}, u32[]{:S(2)}) async-start(bf16[720,8,16]{0,2,1:T(8,128)(2,1)} %bitcast.16), calls=%async_computation.2 | async-start | bytes 393216 | tf_op jit(solution)/shard_map/all_to_all | solution.py:112
  101.6 0.8 convolution_bitcast_fusion.1
  102.4 0.8 fusion.5
  103.2 6.2 %all-to-all-done.1 = bf16[720,8,16]{0,2,1:T(8,128)(2,1)S(1)} async-done(((bf16[720,8,16]{0,2,1:T(8,128)(2,1)}), bf16[720,8,16]{0,2,1:T(8,128)(2,1)S(1)}, u32[]{:S(2)}, u32[]{:S(2)}) %all-to-all-start.1) | async-done | bytes 184352 | tf_op jit(solution)/shard_map/all_to_all | solution.py:112
  109.4 4.0 %gather_fusion.1 = bf16[1024,720]{1,0:T(8,128)(2,1)S(1)} fusion(bf16[720,128]{0,1:T(8,128)(2,1)S(1)} %bitcast.87, s32[1024]{0:T(1024)S(1)} %broadcast_clamp_fusion), kind=kCustom, calls=%fused_computation.1 | custom fusion | bytes 2953216 | tf_op jit(solution)/shard_map/gather | solution.py:115
  113.4 1.9 %convert_bitcast_fusion = f32[720,1024]{0,1:T(8,128)} fusion(bf16[1024,720]{1,0:T(8,128)(2,1)S(1)} %gather_fusion.1), kind=kLoop, calls=%fused_computation.9 | loop fusion | flops 737280 | bytes 4423680 | tf_op jit(solution)/shard_map/convert_element_type | solution.py:116
  115.3 3.1 %reshape.238 = f32[720,256,4]{0,2,1:T(4,128)S(1)} reshape(f32[720,1024]{0,1:T(8,128)} %convert_bitcast_fusion) | data formatting | bytes 5898240 | tf_op jit(solution)/shard_map/convert_element_type | solution.py:116
  118.4 2.7 %multiply_reduce_fusion = bf16[720,256]{0,1:T(8,128)(2,1)} fusion(f32[720,256,4]{0,2,1:T(4,128)S(1)} %reshape.238, f32[256,4]{1,0:T(8,128)S(1)} %copy.82), kind=kLoop, calls=%fused_computation.10 | loop fusion | flops 1290240 | bytes 3321856 | tf_op jit(solution)/shard_map/reduce_sum | solution.py:120
  121.1 1.9 %copy.85 = bf16[256,720]{0,1:T(8,128)(2,1)} copy(bf16[256,720]{1,0:T(8,128)(2,1)} %bitcast.95) | data formatting | bytes 737280
  (55 shorter events, 3.5 us)
Async XLA Ops:
  7.2 78.1 %copy-start = (bf16[1,16,720]{2,1,0:T(8,128)(2,1)S(1)}, bf16[1,16,720]{2,1,0:T(8,128)(2,1)}, u32[]{:S(2)}) copy-start(bf16[1,16,720]{2,1,0:T(8,128)(2,1)} %param.19) | copy-start | bytes 69124
  7.2 24.9 %all-gather.2.cloned.1.call-start = ((), (), s32[]{:S(2)}) async-start(), calls=%async_computation.4 | async-start | bytes 1843200 | tf_op jit(solution)/shard_map/all_gather | solution.py:76
  9.0 11.9 %copy-start.2 = (f32[1,2,720,90]{2,1,3,0:T(2,128)S(1)}, f32[1,2,720,90]{2,1,3,0:T(2,128)}, u32[]{:S(2)}) copy-start(f32[1,2,720,90]{2,1,3,0:T(2,128)} %param.15) | copy-start | bytes 1555204
  9.0 15.0 %copy-start.7 = (f32[256,4]{0,1:T(4,128)S(1)}, f32[256,4]{0,1:T(4,128)}, u32[]{:S(2)}) copy-start(f32[256,4]{0,1:T(4,128)} %param.13) | copy-start | bytes 12292
  25.5 6.6 %copy-start.4 = (f32[1,720,90]{1,0,2:T(1,128)S(1)}, f32[1,720,90]{1,0,2:T(1,128)}, u32[]{:S(2)}) copy-start(f32[1,720,90]{1,0,2:T(1,128)} %param.17) | copy-start | bytes 777604
  36.1 26.9 %all-to-all-start = ((bf16[8,16,2880]{2,1,0:T(8,128)(2,1)}), bf16[8,16,2880]{2,1,0:T(8,128)(2,1)S(1)}, u32[]{:S(2)}, u32[]{:S(2)}) async-start(bf16[8,16,2880]{2,1,0:T(8,128)(2,1)} %broadcast_select_fusion), calls=%async_computation | async-start | bytes 1507328 | tf_op jit(solution)/shard_map/all_to_all | solution.py:81
  43.3 50.8 %reduce-scatter.2.cloned.1.call-start = ((), (), s32[]{:S(2)}) async-start(), calls=%async_computation.5 | async-start | bytes 921600 | tf_op jit(solution)/shard_map/reduce_scatter | solution.py:100
  62.9 6.6 %copy-start.1 = (bf16[720,90,32]{0,2,1:T(8,128)(2,1)S(1)}, bf16[720,90,32]{0,2,1:T(8,128)(2,1)}, u32[]{:S(2)}) copy-start(bf16[720,90,32]{0,2,1:T(8,128)(2,1)} %fusion.1) | copy-start | bytes 12441604
  69.3 2.4 %copy-start.3 = (bf16[256,720]{0,1:T(8,128)(2,1)S(1)}, bf16[256,720]{0,1:T(8,128)(2,1)}, u32[]{:S(2)}) copy-start(bf16[256,720]{0,1:T(8,128)(2,1)} %param.11) | copy-start | bytes 1105924
  69.5 8.1 %copy-start.5 = (s32[256,4]{0,1:T(4,128)S(1)}, s32[256,4]{0,1:T(4,128)}, u32[]{:S(2)}) copy-start(s32[256,4]{0,1:T(4,128)} %param.12) | copy-start | bytes 12292
  69.5 15.9 %copy-start.6 = (bf16[1,720,16]{1,2,0:T(8,128)(2,1)S(1)}, bf16[1,720,16]{1,2,0:T(8,128)(2,1)}, u32[]{:S(2)}) copy-start(bf16[1,720,16]{1,2,0:T(8,128)(2,1)} %param.18) | copy-start | bytes 69124
  73.6 11.7 %all-to-all-start.2 = ((bf16[8,16,720]{2,1,0:T(8,128)(2,1)}), bf16[8,16,720]{2,1,0:T(8,128)(2,1)S(1)}, u32[]{:S(2)}, u32[]{:S(2)}) async-start(bf16[8,16,720]{2,1,0:T(8,128)(2,1)} %fusion.7), calls=%async_computation.3 | async-start | bytes 393216 | tf_op jit(solution)/shard_map/all_to_all | solution.py:82
  96.1 13.3 %all-to-all-start.1 = ((bf16[720,8,16]{0,2,1:T(8,128)(2,1)}), bf16[720,8,16]{0,2,1:T(8,128)(2,1)S(1)}, u32[]{:S(2)}, u32[]{:S(2)}) async-start(bf16[720,8,16]{0,2,1:T(8,128)(2,1)} %bitcast.16), calls=%async_computation.2 | async-start | bytes 393216 | tf_op jit(solution)/shard_map/all_to_all | solution.py:112
Sparse Core Ops, SparseCore 0:
  9.6 21.7 all-gather.1
  71.9 22.1 reduce-scatter.1
where the time goes:
time: 131 us; the launch traced here: 130 us
  local copies, waits for them, and re-layouts  35.9 us (27%)
  other arithmetic  25.7 us (20%)
  waiting for transfers between devices  19.6 us (15%)
  starting transfers between devices  16.4 us (13%)
  between operations  14.3 us (11%)
  matrix products  11.7 us (9%)
  blocking collectives  6.32 us (5%)
    unnamed x23, local copies, waits for them, and re-layouts  21.5 us
    convert_element_type x1, other arithmetic, dequant_gate_up(): (shaped * scales[:, :, :, None]).reshape(pair, hidden, width)  10.4 us
    all_to_all x1, waiting for transfers between devices, on_device(): lax.all_to_all(gradient_rows, 'ctx', split_axis=0, concat_axis=0, tiled=T...  7.33 us
    all_to_all x1, starting transfers between devices, on_device(): lax.all_to_all(row_data, 'ctx', split_axis=0, concat_axis=0, tiled=True)  7.25 us
    dot_general x1, matrix products, on_device(): jnp.einsum('sn,cfn->csf', got_rows, w_joined, preferred_element_type=jnp....  6.39 us
    psum x1, blocking collectives, on_device(): lax.psum(low_term.astype(jnp.bfloat16), 'exp').astype(jnp.float32)  6.32 us
    all_to_all x1, waiting for transfers between devices, on_device(): lax.all_to_all(output_columns, 'ctx', split_axis=1, concat_axis=1, tiled=...  6.2 us
    convert_element_type x1, other arithmetic, dequant_down(): (shaped * scales[:, :, None]).reshape(hidden, width).astype(jnp.bfloat16)  5.85 us
  transfers between devices with their start and end apart: 5, of which 4 were waited for; matrix products, arithmetic and copies ran while one was open for 35% of the time, Pallas kernels for 0%

commit v1 on v0

v1 whole, which is shorter than its diff:
```python
import functools

import jax
import jax.numpy as jnp
from jax import lax
from jax.experimental import pallas as pl
from jax.experimental.pallas import tpu as pltpu
from jax.sharding import PartitionSpec as P

CAP = 16
BLOCK = 32
ADAPTER_SCALE = 0.5
GLU_ALPHA = 1.702
CLAMP_LIMIT = 7.0

F32 = jnp.float32
BF16 = jnp.bfloat16
NN = (((1,), (0,)), ((), ()))
NT = (((1,), (1,)), ((), ()))
TN = (((0,), (0,)), ((), ()))


def dot(a, b, dims):
    return lax.dot_general(a, b, dims, preferred_element_type=F32)


def unit_rows(hidden):
    for rows in (240, 144, 128, 80, 48, 16):
        if hidden % rows == 0:
            return rows
    return hidden


def block_kernel(
    C, F,
    tok_h, cot_h, idx_h, rw_h, gu_h, gus_h, dn_h, dns_h, adl_h, adu_h,
    out_h, lg_h, rg_h,
    tok, cot, idx, rw, raw, gus, dns, adl, adu,
    spad, ssc, expand, rows, grows, xin, gin, xfull, wd,
    base, part, pair, tosend, fromy, rank_b, rank_l, outrows, ret,
    out_v, lg_v, rg_v,
    load, store, tS, tR, gS, gR, rS, rR, yS, yR, kS, kR, bS, bR, lS, lR, pS, pR, qS, qR,
):
    NY = F // 2
    H, width = raw.shape[1], raw.shape[2]
    feat = tok.shape[0]
    T = tok.shape[1]
    R = C * CAP
    NB = width // BLOCK
    c = lax.axis_index("ctx")
    f = lax.axis_index("exp")
    y = f // 2
    q = f % 2
    mate = f + 1 - 2 * q

    def at_ctx(other):
        return dict(device_id=(other, f), device_id_type=pl.DeviceIdType.MESH)

    def at_exp(other):
        return dict(device_id=(c, other), device_id_type=pl.DeviceIdType.MESH)

    barrier = pltpu.get_barrier_semaphore()

    @pl.loop(1, C)
    def _(i):
        pl.semaphore_signal(barrier, inc=1, **at_ctx(lax.rem(c + i, C)))

    @pl.loop(1, F)
    def _(i):
        pl.semaphore_signal(barrier, inc=1, **at_exp(lax.rem(f + i, F)))

    loads = [
        pltpu.make_async_copy(idx_h, idx, load.at[0]),
        pltpu.make_async_copy(tok_h, tok, load.at[1]),
        pltpu.make_async_copy(rw_h, rw, load.at[2]),
        pltpu.make_async_copy(cot_h, cot, load.at[3]),
        pltpu.make_async_copy(gus_h, gus, load.at[4]),
        pltpu.make_async_copy(dns_h, dns, load.at[5]),
        pltpu.make_async_copy(gu_h.at[0], raw.at[0], load.at[6]),
        pltpu.make_async_copy(gu_h.at[1], raw.at[1], load.at[7]),
        pltpu.make_async_copy(dn_h, raw.at[2], load.at[8]),
        pltpu.make_async_copy(adl_h, adl, load.at[9]),
        pltpu.make_async_copy(adu_h, adu, load.at[10]),
    ]
    for copy in loads:
        copy.start()

    loads[0].wait()
    slot = lax.broadcasted_iota(jnp.int32, (R, T), 0)
    expert = lax.shift_right_logical(slot, 4)
    number = lax.bitwise_and(slot, 15).astype(F32)
    named = idx[0:1, :] == expert
    for k in range(1, idx.shape[0]):
        named = jnp.logical_or(named, idx[k:k + 1, :] == expert)
    earlier = (
        lax.broadcasted_iota(jnp.int32, (T, T), 0) < lax.broadcasted_iota(jnp.int32, (T, T), 1)
    ).astype(F32).astype(BF16)
    position = dot(named.astype(F32).astype(BF16), earlier, NN)
    hit = jnp.logical_and(named, position == number)
    pick = hit.astype(F32).astype(BF16)
    loads[1].wait()
    rows[...] = dot(pick, tok[...], NT).astype(BF16).reshape(C, CAP, feat)

    pl.semaphore_wait(barrier, C - 1 + F - 1)

    def send_rows(src, dst, ss, rs, other, **where):
        return pltpu.make_async_remote_copy(
            src_ref=src, dst_ref=dst, send_sem=ss, recv_sem=rs, **where
        )

    def tok_copy(other, came):
        return send_rows(rows.at[other], xin.at[f, came], tS.at[other], tR.at[came], other, **at_ctx(other))

    def grad_copy(other, came):
        return send_rows(grows.at[other], gin.at[came], gS.at[other], gR.at[came], other, **at_ctx(other))

    def ret_copy(other, came):
        return send_rows(outrows.at[other], ret.at[came], rS.at[other], rR.at[came], other, **at_ctx(other))

    def y_copy(b, yy, came):
        return send_rows(
            xin.at[2 * came + q, b], xin.at[2 * came + q, b], yS.at[yy, b], yR.at[came, b], 0,
            **at_exp(2 * yy + q),
        )

    def k_copy(yy, b, core):
        return send_rows(
            xin.at[2 * yy + core, b], xin.at[2 * yy + core, b], kS.at[yy, b], kR.at[yy, b], 0,
            **at_exp(mate),
        )

    @pl.loop(1, C)
    def _(i):
        other = lax.rem(c + i, C)
        tok_copy(other, c).start()

    xin[f, c] = rows[c]

    loads[2].wait()
    weight = jnp.zeros((R, T), F32)
    for k in range(idx.shape[0]):
        weight = weight + jnp.where(idx[k:k + 1, :] == expert, rw[k:k + 1, :], 0.0)
    weight = jnp.where(hit, weight, 0.0)
    wd[...] = weight
    loads[3].wait()
    picked = dot(pick, cot[...], NT) * jnp.sum(weight, axis=1, keepdims=True)
    grows[...] = picked.astype(BF16).reshape(C, CAP, feat)

    @pl.loop(1, C)
    def _(i):
        other = lax.rem(c + i, C)
        grad_copy(other, c).start()

    gin[c] = grows[c]

    expand[...] = (
        lax.shift_right_logical(lax.broadcasted_iota(jnp.int32, expand.shape, 1), 5)
        == lax.broadcasted_iota(jnp.int32, expand.shape, 0)
    ).astype(F32).astype(BF16)
    spad[...] = jnp.zeros_like(spad)
    loads[4].wait()
    loads[5].wait()
    for m in range(3):
        if m < 2:
            spad[0:NB, 0:H] = gus[:, m, :]
        else:
            spad[0:NB, 0:H] = dns[:, 0, :]
        ssc[m] = jnp.transpose(spad[...]).astype(BF16)[0:H]
    for i in (6, 7, 8):
        loads[i].wait()

    unit = unit_rows(H)
    per = H // unit
    lanes = 256

    def dequant(u):
        m = u // per
        at = pl.ds(pl.multiple_of(lax.rem(u, per) * unit, unit), unit) if per > 1 else slice(None)
        scale = ssc[m, at, :]
        for lo in range(0, width, lanes):
            hi = min(lo + lanes, width)
            spread = dot(scale, expand[:, lo:hi], NN).astype(BF16)
            raw[m, at, lo:hi] = raw[m, at, lo:hi] * spread

    def forward(i):
        b = lax.rem(c - i + C, C)

        @pl.when(i > 0)
        def _():
            tok_copy(b, b).wait_recv()

        @pl.loop(1, NY)
        def _(j):
            y_copy(b, lax.rem(y + j, NY), y).start()

        k_copy(y, b, q).start()

    units = 3 * per
    groups = -(-C // units)

    @pl.loop(0, units)
    def _(u):
        @pl.loop(0, groups)
        def _(g):
            i = u * groups + g

            @pl.when(i < C)
            def _():
                forward(i)

        dequant(u)

    @pl.loop(1, NY)
    def _(j):
        yy = lax.rem(y - j + NY, NY)

        @pl.loop(0, C)
        def _(i):
            b = lax.rem(c - i + C, C)
            y_copy(b, y, yy).wait_recv()
            k_copy(yy, b, q).start()

    @pl.loop(1, C)
    def _(i):
        b = lax.rem(c - i + C, C)
        grad_copy(b, b).wait_recv()

    loads[9].wait()
    loads[10].wait()
    grads = gin[...].reshape(R, feat)
    right = adu[...]
    rank_b[f] = dot(right, grads, NT).astype(BF16)

    def rank_copy(buf, ss, rs, other, came):
        return send_rows(buf.at[came], buf.at[came], ss.at[other], rs.at[came], other, **at_exp(other))

    @pl.loop(1, F)
    def _(j):
        rank_copy(rank_b, bS, bR, lax.rem(f + j, F), f).start()

    @pl.loop(0, NY)
    def _(yy):
        @pl.loop(0, C)
        def _(b):
            k_copy(yy, b, 1 - q).wait_recv()

    for g in range(F):
        xfull[:, g * feat:(g + 1) * feat] = xin[g].reshape(R, feat)
    x = xfull[...]
    gate = jnp.minimum(dot(x, raw[0], NT), CLAMP_LIMIT)
    up = jnp.clip(dot(x, raw[1], NT), -CLAMP_LIMIT, CLAMP_LIMIT)
    activated = ((up + 1.0) * gate / (1.0 + jnp.exp(-GLU_ALPHA * gate))).astype(BF16)

    rank_l[f] = dot(adl[...], activated, NT).astype(BF16)

    @pl.loop(1, F)
    def _(j):
        rank_copy(rank_l, lS, lR, lax.rem(f + j, F), f).start()

    base[...] = dot(activated, raw[2], NN)
    for g in range(F):
        part[g] = base[:, g * feat:(g + 1) * feat].astype(BF16)

    def pair_copy(yy, core):
        return send_rows(
            part.at[2 * yy + core], pair.at[yy], pS.at[yy], pR.at[yy], 0, **at_exp(mate)
        )

    def sum_copy(yy, came):
        return send_rows(tosend.at[yy], fromy.at[came], qS.at[yy], qR.at[came], 0, **at_exp(2 * yy + q))

    @pl.loop(1, NY + 1)
    def _(j):
        pair_copy(lax.rem(y + j, NY), 1 - q).start()

    @pl.loop(1, NY)
    def _(j):
        yy = lax.rem(y + j, NY)
        pair_copy(yy, q).wait_recv()
        tosend[yy] = (part[2 * yy + q].astype(F32) + pair[yy].astype(F32)).astype(BF16)
        sum_copy(yy, y).start()

    @pl.loop(1, F)
    def _(j):
        other = lax.rem(f - j + F, F)
        rank_copy(rank_b, bS, bR, other, other).wait_recv()
        rank_copy(rank_l, lS, lR, other, other).wait_recv()

    low = rank_l[0].astype(F32)
    back = rank_b[0].astype(F32)
    for g in range(1, F):
        low = low + rank_l[g].astype(F32)
        back = back + rank_b[g].astype(F32)
    low = low.astype(BF16)
    back = (ADAPTER_SCALE * back).astype(BF16)
    lg_v[...] = dot(back, activated, NN)
    rg_v[...] = ADAPTER_SCALE * dot(low, grads, NN)
    pltpu.make_async_copy(lg_v, lg_h, store.at[0]).start()
    pltpu.make_async_copy(rg_v, rg_h, store.at[1]).start()
    adapted = ADAPTER_SCALE * dot(low, right, TN)

    pair_copy(y, q).wait_recv()
    total = part[f].astype(F32) + pair[y].astype(F32) + adapted
    base[:, 0:feat] = total

    @pl.loop(1, NY)
    def _(j):
        yy = lax.rem(y - j + NY, NY)
        sum_copy(y, yy).wait_recv()
        base[:, 0:feat] += fromy[yy].astype(F32)

    outrows[...] = base[:, 0:feat].astype(BF16).reshape(C, CAP, feat)

    @pl.loop(1, C)
    def _(i):
        other = lax.rem(c + i, C)
        ret_copy(other, c).start()

    ret[c] = outrows[c]

    @pl.loop(1, C)
    def _(i):
        other = lax.rem(c + i, C)
        tok_copy(other, c).wait_send()
        grad_copy(other, c).wait_send()

    @pl.loop(0, C)
    def _(b):
        @pl.loop(1, NY)
        def _(j):
            y_copy(b, lax.rem(y + j, NY), y).wait_send()

        @pl.loop(0, NY)
        def _(yy):
            k_copy(yy, b, q).wait_send()

    @pl.loop(1, F)
    def _(j):
        other = lax.rem(f + j, F)
        rank_copy(rank_b, bS, bR, other, f).wait_send()
        rank_copy(rank_l, lS, lR, other, f).wait_send()

    @pl.loop(0, NY)
    def _(yy):
        pair_copy(yy, 1 - q).wait_send()

    @pl.loop(1, NY)
    def _(j):
        sum_copy(lax.rem(y + j, NY), y).wait_send()

    wfull = wd[...]
    whigh = wfull.astype(BF16)
    wlow = (wfull - whigh.astype(F32)).astype(BF16)

    @pl.loop(1, C)
    def _(i):
        b = lax.rem(c - i + C, C)
        ret_copy(b, b).wait_recv()

    back_rows = ret[...].reshape(R, feat)
    out_v[...] = (dot(back_rows, whigh, TN) + dot(back_rows, wlow, TN)).astype(BF16)
    pltpu.make_async_copy(out_v, out_h, store.at[2]).start()

    @pl.loop(1, C)
    def _(i):
        other = lax.rem(c + i, C)
        ret_copy(other, c).wait_send()

    pltpu.make_async_copy(lg_v, lg_h, store.at[0]).wait()
    pltpu.make_async_copy(rg_v, rg_h, store.at[1]).wait()
    pltpu.make_async_copy(out_v, out_h, store.at[2]).wait()


def on_device(
    tokens,
    cotangent,
    expert_indices,
    routing_weights,
    gate_up_weight_blocks,
    gate_up_block_scales,
    down_weight_blocks,
    down_block_scales,
    adapter_down_matrix,
    adapter_up_matrix,
):
    C = lax.axis_size("ctx")
    F = lax.axis_size("exp")
    NY = F // 2
    T, feat = tokens.shape
    top = expert_indices.shape[1]
    _, H, width = down_weight_blocks.shape
    rank = adapter_up_matrix.shape[1]
    R = C * CAP
    NB = width // BLOCK
    hpad = -(-H // 128) * 128
    bpad = -(-NB // 128) * 128
    dma = pltpu.SemaphoreType.DMA
    scratch = [
        pltpu.VMEM((feat, T), BF16),
        pltpu.VMEM((feat, T), BF16),
        pltpu.VMEM((top, T), jnp.int32),
        pltpu.VMEM((top, T), F32),
        pltpu.VMEM((3, H, width), BF16),
        pltpu.VMEM((NB, 2, H), F32),
        pltpu.VMEM((NB, 1, H), F32),
        pltpu.VMEM((rank, H), BF16),
        pltpu.VMEM((rank, feat), BF16),
        pltpu.VMEM((bpad, hpad), F32),
        pltpu.VMEM((3, H, bpad), BF16),
        pltpu.VMEM((bpad, width), BF16),
        pltpu.VMEM((C, CAP, feat), BF16),
        pltpu.VMEM((C, CAP, feat), BF16),
        pltpu.VMEM((F, C, CAP, feat), BF16),
        pltpu.VMEM((C, CAP, feat), BF16),
        pltpu.VMEM((R, width), BF16),
        pltpu.VMEM((R, T), F32),
        pltpu.VMEM((R, width), F32),
        pltpu.VMEM((F, R, feat), BF16),
        pltpu.VMEM((NY, R, feat), BF16),
        pltpu.VMEM((NY, R, feat), BF16),
        pltpu.VMEM((NY, R, feat), BF16),
        pltpu.VMEM((F, rank, R), BF16),
        pltpu.VMEM((F, rank, R), BF16),
        pltpu.VMEM((C, CAP, feat), BF16),
        pltpu.VMEM((C, CAP, feat), BF16),
        pltpu.VMEM((feat, T), BF16),
        pltpu.VMEM((rank, H), F32),
        pltpu.VMEM((rank, feat), F32),
        dma((11,)), dma((3,)),
        dma((C,)), dma((C,)), dma((C,)), dma((C,)), dma((C,)), dma((C,)),
        dma((NY, C)), dma((NY, C)), dma((NY, C)), dma((NY, C)),
        dma((F,)), dma((F,)), dma((F,)), dma((F,)),
        dma((NY,)), dma((NY,)), dma((NY,)), dma((NY,)),
    ]
    any_space = pl.BlockSpec(memory_space=pl.ANY)
    out_t, left_t, right = pl.pallas_call(
        functools.partial(block_kernel, C, F),
        out_shape=(
            jax.ShapeDtypeStruct((feat, T), BF16),
            jax.ShapeDtypeStruct((rank, H), F32),
            jax.ShapeDtypeStruct((rank, feat), F32),
        ),
        in_specs=[any_space] * 10,
        out_specs=(any_space,) * 3,
        scratch_shapes=scratch,
        compiler_params=pltpu.CompilerParams(
            collective_id=0, has_side_effects=True, vmem_limit_bytes=52 * 2**20
        ),
    )(
        tokens.T,
        cotangent.T,
        expert_indices.T,
        routing_weights.T,
        gate_up_weight_blocks[0],
        jnp.transpose(gate_up_block_scales[0], (2, 0, 1)),
        down_weight_blocks[0],
        jnp.transpose(down_block_scales, (2, 0, 1)),
        adapter_down_matrix[0].T,
        adapter_up_matrix[0],
    )
    return out_t.T, left_t.T[None], right[None]


def solution(mesh):
    placed = (
        P("ctx", "exp"),
        P("ctx", "exp"),
        P("ctx", None),
        P("ctx", None),
        P("ctx", None, "exp", None),
        P("ctx", None, "exp", None),
        P("ctx", "exp", None),
        P("ctx", "exp", None),
        P("ctx", "exp", None),
        P("ctx", None, "exp"),
    )
    return jax.shard_map(
        on_device,
        mesh=mesh,
        in_specs=placed,
        out_specs=(P("ctx", "exp"), P("ctx", "exp", None), P("ctx", None, "exp")),
        check_vma=False,
    )
```

time: 131 us -> 45.8 us (0.35)
  Pallas kernels: 0 us -> 37 us
  local copies, waits for them, and re-layouts: 35.9 us -> 7.75 us
  other arithmetic: 25.7 us -> 0 us
  waiting for transfers between devices: 19.6 us -> 0 us
  starting transfers between devices: 16.4 us -> 0 us
  between operations: 14.3 us -> 0.66 us
  matrix products: 11.7 us -> 0 us
  blocking collectives: 6.32 us -> 0 us
    pallas_call x0 -> x1, Pallas kernels: none -> 37 us  [on_device(): pl.pallas_call(functools.partial(block_kernel, C, F), out_shape=(jax.Shap...]
    convert_element_type x6 -> x0, other arithmetic: 19 us -> none  [the longest x1 10.4 us: dequant_gate_up(): (shaped * scales[:, :, :, None]).reshape(pair, hidden, width)]
    all_to_all x3 -> x0, waiting for transfers between devices: 16.7 us -> none  [the longest x1 7.33 us: on_device(): lax.all_to_all(gradient_rows, 'ctx', split_axis=0, concat_axis=0, tiled=T...]
    all_to_all x3 -> x0, starting transfers between devices: 16.2 us -> none  [the longest x1 7.25 us: on_device(): lax.all_to_all(row_data, 'ctx', split_axis=0, concat_axis=0, tiled=True)]
    unnamed x23 -> x17, local copies, waits for them, and re-layouts: 21.5 us -> 7.75 us
    dot_general x7 -> x0, matrix products: 11.7 us -> none  [the longest x1 6.39 us: on_device(): jnp.einsum('sn,cfn->csf', got_rows, w_joined, preferred_element_type=jnp....]
    gather x5 -> x0, local copies, waits for them, and re-layouts: 6.97 us -> none  [the longest x1 4 us: on_device(): returned[:, safe_index].astype(jnp.float32)]
    psum x1 -> x0, blocking collectives: 6.32 us -> none  [on_device(): lax.psum(low_term.astype(jnp.bfloat16), 'exp').astype(jnp.float32)]
  transfers between devices with their start and end apart: 5 -> 0, of which waited for: 4 -> 0; matrix products, arithmetic and copies ran while one was open for 35% -> 0% of each run, Pallas kernels for 0% -> 0%
where the time goes in v1:
time: 45.8 us; the launch traced here: 45.4 us
  Pallas kernels  37 us (81%)
  local copies, waits for them, and re-layouts  7.75 us (17%)
  between operations  0.66 us (1%)
    pallas_call x1, Pallas kernels, on_device(): pl.pallas_call(functools.partial(block_kernel, C, F), out_shape=(jax.Shap...  37 us
    unnamed x17, local copies, waits for them, and re-layouts  7.75 us

profile of v1, /device:TPU:0, one launch (start us, length us, event | category | flops | bytes accessed | tf_op | source)
XLA Modules:
  0.0 45.4 jit_solution(7385672095163369685)
XLA Ops:
  0.6 0.0 copy-start
  0.6 1.0 %copy-done = bf16[256,720]{0,1:T(8,128)(2,1)S(1)} copy-done((bf16[256,720]{0,1:T(8,128)(2,1)S(1)}, bf16[256,720]{0,1:T(8,128)(2,1)}, u32[]{:S(2)}) %copy-start) | copy-done | bytes 368664
  1.6 0.0 copy-start.1
  1.6 1.0 %copy-done.1 = bf16[256,720]{0,1:T(8,128)(2,1)S(1)} copy-done((bf16[256,720]{0,1:T(8,128)(2,1)S(1)}, bf16[256,720]{0,1:T(8,128)(2,1)}, u32[]{:S(2)}) %copy-start.1) | copy-done | bytes 368664
  2.6 0.0 copy-start.2
  2.6 1.0 %copy-done.2 = f32[1,720,90]{1,0,2:T(1,128)S(1)} copy-done((f32[1,720,90]{1,0,2:T(1,128)S(1)}, f32[1,720,90]{1,0,2:T(1,128)}, u32[]{:S(2)}) %copy-start.2) | copy-done | bytes 259224
  3.6 0.0 copy-start.3
  3.6 0.7 %copy-done.3 = bf16[1,720,16]{1,2,0:T(8,128)(2,1)S(1)} copy-done((bf16[1,720,16]{1,2,0:T(8,128)(2,1)S(1)}, bf16[1,720,16]{1,2,0:T(8,128)(2,1)}, u32[]{:S(2)}) %copy-start.3) | copy-done | bytes 23064
  4.3 0.0 copy-start.4
  4.3 0.7 %copy-done.4 = bf16[1,16,720]{2,1,0:T(8,128)(2,1)S(1)} copy-done((bf16[1,16,720]{2,1,0:T(8,128)(2,1)S(1)}, bf16[1,16,720]{2,1,0:T(8,128)(2,1)}, u32[]{:S(2)}) %copy-start.4) | copy-done | bytes 23064
  5.0 0.0 copy-start.5
  5.0 0.7 %copy-done.5 = s32[256,4]{0,1:T(4,128)S(1)} copy-done((s32[256,4]{0,1:T(4,128)S(1)}, s32[256,4]{0,1:T(4,128)}, u32[]{:S(2)}) %copy-start.5) | copy-done | bytes 4120
  5.7 0.0 copy-start.6
  5.7 0.7 %copy-done.6 = f32[256,4]{0,1:T(4,128)S(1)} copy-done((f32[256,4]{0,1:T(4,128)S(1)}, f32[256,4]{0,1:T(4,128)}, u32[]{:S(2)}) %copy-start.6) | copy-done | bytes 4120
  6.4 37.0 %shard_map.121 = (bf16[720,256]{1,0:T(8,128)(2,1)S(1)}, f32[16,720]{1,0:T(8,128)S(1)}, f32[16,720]{1,0:T(8,128)S(1)}) custom-call(bf16[720,256]{1,0:T(8,128)(2,1)S(1)} %bitcast.19, bf16[720,256]{1,0:T(8,128)(2,1)S(1)} %bitcast.20, s32[4,256]{1,0:T(4,128)S(1)} %bitcast.27, f32[4,256]{1,0:T(4,128)S(1)} %bitcast.28, bf16[2,720,2880]{2,1,0:T(8,128)(2,1)} %bitcast.29, ...), custom_call_target="tpu_custom_call" | custom-call | tf_op jit(solution)/shard_map/pallas_call | solution.py:436
  43.4 0.7 %copy.16 = bf16[256,720]{0,1:T(8,128)(2,1)} copy(bf16[256,720]{0,1:T(8,128)(2,1)S(1)} %bitcast.21) | data formatting | bytes 737280
  44.2 0.6 %copy.17 = f32[1,720,16]{1,2,0:T(8,128)} copy(f32[1,720,16]{1,2,0:T(8,128)S(1)} %bitcast.24) | data formatting | bytes 92160
  44.8 0.6 %copy.18 = f32[1,16,720]{2,1,0:T(8,128)} copy(f32[1,16,720]{2,1,0:T(8,128)S(1)} %bitcast.23) | data formatting | bytes 92160
Async XLA Ops:
  0.6 1.0 %copy-start = (bf16[256,720]{0,1:T(8,128)(2,1)S(1)}, bf16[256,720]{0,1:T(8,128)(2,1)}, u32[]{:S(2)}) copy-start(bf16[256,720]{0,1:T(8,128)(2,1)} %param.10) | copy-start | bytes 1105924
  1.6 1.0 %copy-start.1 = (bf16[256,720]{0,1:T(8,128)(2,1)S(1)}, bf16[256,720]{0,1:T(8,128)(2,1)}, u32[]{:S(2)}) copy-start(bf16[256,720]{0,1:T(8,128)(2,1)} %param.11) | copy-start | bytes 1105924
  2.6 1.0 %copy-start.2 = (f32[1,720,90]{1,0,2:T(1,128)S(1)}, f32[1,720,90]{1,0,2:T(1,128)}, u32[]{:S(2)}) copy-start(f32[1,720,90]{1,0,2:T(1,128)} %param.17) | copy-start | bytes 777604
  3.6 0.7 %copy-start.3 = (bf16[1,720,16]{1,2,0:T(8,128)(2,1)S(1)}, bf16[1,720,16]{1,2,0:T(8,128)(2,1)}, u32[]{:S(2)}) copy-start(bf16[1,720,16]{1,2,0:T(8,128)(2,1)} %param.18) | copy-start | bytes 69124
  4.3 0.7 %copy-start.4 = (bf16[1,16,720]{2,1,0:T(8,128)(2,1)S(1)}, bf16[1,16,720]{2,1,0:T(8,128)(2,1)}, u32[]{:S(2)}) copy-start(bf16[1,16,720]{2,1,0:T(8,128)(2,1)} %param.19) | copy-start | bytes 69124
  5.0 0.7 %copy-start.5 = (s32[256,4]{0,1:T(4,128)S(1)}, s32[256,4]{0,1:T(4,128)}, u32[]{:S(2)}) copy-start(s32[256,4]{0,1:T(4,128)} %param.12) | copy-start | bytes 12292
  5.7 0.7 %copy-start.6 = (f32[256,4]{0,1:T(4,128)S(1)}, f32[256,4]{0,1:T(4,128)}, u32[]{:S(2)}) copy-start(f32[256,4]{0,1:T(4,128)} %param.13) | copy-start | bytes 12292

commit v2 on v1

--- a/solution.py
+++ b/solution.py
@@ -34,12 +34,11 @@
 def block_kernel(
     C, F,
     tok_h, cot_h, idx_h, rw_h, gu_h, gus_h, dn_h, dns_h, adl_h, adu_h,
-    out_h, lg_h, rg_h,
+    ret, wd, lg_v, rg_v,
     tok, cot, idx, rw, raw, gus, dns, adl, adu,
-    spad, ssc, expand, rows, grows, xin, gin, xfull, wd,
-    base, part, pair, tosend, fromy, rank_b, rank_l, outrows, ret,
-    out_v, lg_v, rg_v,
-    load, store, tS, tR, gS, gR, rS, rR, yS, yR, kS, kR, bS, bR, lS, lR, pS, pR, qS, qR,
+    spad, ssc, expand, rows, grows, xin, gin, xfull,
+    base, part, pair, tosend, fromy, rank_b, rank_l, outrows, adapt,
+    load, tS, tR, gS, gR, rS, rR, yS, yR, kS, kR, bS, bR, lS, lR, pS, pR, qS, qR,
 ):
     NY = F // 2
     H, width = raw.shape[1], raw.shape[2]
@@ -146,13 +145,6 @@
     picked = dot(pick, cot[...], NT) * jnp.sum(weight, axis=1, keepdims=True)
     grows[...] = picked.astype(BF16).reshape(C, CAP, feat)
 
-    @pl.loop(1, C)
-    def _(i):
-        other = lax.rem(c + i, C)
-        grad_copy(other, c).start()
-
-    gin[c] = grows[c]
-
     expand[...] = (
         lax.shift_right_logical(lax.broadcasted_iota(jnp.int32, expand.shape, 1), 5)
         == lax.broadcasted_iota(jnp.int32, expand.shape, 0)
@@ -166,9 +158,6 @@
         else:
             spad[0:NB, 0:H] = dns[:, 0, :]
         ssc[m] = jnp.transpose(spad[...]).astype(BF16)[0:H]
-    for i in (6, 7, 8):
-        loads[i].wait()
-
     unit = unit_rows(H)
     per = H // unit
     lanes = 256
@@ -195,54 +184,49 @@
 
         k_copy(y, b, q).start()
 
+    def y_forward(i):
+        yy = lax.rem(y - 1 - i // C + NY, NY)
+        b = lax.rem(c - lax.rem(i, C) + C, C)
+        y_copy(b, y, yy).wait_recv()
+        k_copy(yy, b, q).start()
+
     units = 3 * per
-    groups = -(-C // units)
-
-    @pl.loop(0, units)
-    def _(u):
-        @pl.loop(0, groups)
-        def _(g):
-            i = u * groups + g
-
-            @pl.when(i < C)
+    events = NY * C
+
+    @pl.loop(0, max(events, units))
+    def _(s):
+        for m in range(3):
+            @pl.when(s == m * per)
             def _():
-                forward(i)
-
-        dequant(u)
-
-    @pl.loop(1, NY)
-    def _(j):
-        yy = lax.rem(y - j + NY, NY)
-
-        @pl.loop(0, C)
-        def _(i):
-            b = lax.rem(c - i + C, C)
-            y_copy(b, y, yy).wait_recv()
-            k_copy(yy, b, q).start()
-
-    @pl.loop(1, C)
-    def _(i):
-        b = lax.rem(c - i + C, C)
-        grad_copy(b, b).wait_recv()
-
-    loads[9].wait()
-    loads[10].wait()
-    grads = gin[...].reshape(R, feat)
-    right = adu[...]
-    rank_b[f] = dot(right, grads, NT).astype(BF16)
-
-    def rank_copy(buf, ss, rs, other, came):
-        return send_rows(buf.at[came], buf.at[came], ss.at[other], rs.at[came], other, **at_exp(other))
-
-    @pl.loop(1, F)
-    def _(j):
-        rank_copy(rank_b, bS, bR, lax.rem(f + j, F), f).start()
+                loads[6 + m].wait()
+
+        @pl.when(s < units)
+        def _():
+            dequant(s)
+
+        @pl.when(s < C)
+        def _():
+            forward(s)
+
+        @pl.when(jnp.logical_and(s >= C, s < events))
+        def _():
+            y_forward(s - C)
+
+    @pl.loop(1, C)
+    def _(i):
+        other = lax.rem(c + i, C)
+        grad_copy(other, c).start()
+
+    gin[c] = grows[c]
 
     @pl.loop(0, NY)
     def _(yy):
         @pl.loop(0, C)
         def _(b):
             k_copy(yy, b, 1 - q).wait_recv()
+
+    def rank_copy(buf, ss, rs, other, came):
+        return send_rows(buf.at[came], buf.at[came], ss.at[other], rs.at[came], other, **at_exp(other))
 
     for g in range(F):
         xfull[:, g * feat:(g + 1) * feat] = xin[g].reshape(R, feat)
@@ -251,6 +235,8 @@
     up = jnp.clip(dot(x, raw[1], NT), -CLAMP_LIMIT, CLAMP_LIMIT)
     activated = ((up + 1.0) * gate / (1.0 + jnp.exp(-GLU_ALPHA * gate))).astype(BF16)
 
+    loads[9].wait()
+    loads[10].wait()
     rank_l[f] = dot(adl[...], activated, NT).astype(BF16)
 
     @pl.loop(1, F)
@@ -259,64 +245,104 @@
 
     base[...] = dot(activated, raw[2], NN)
     for g in range(F):
-        part[g] = base[:, g * feat:(g + 1) * feat].astype(BF16)
-
-    def pair_copy(yy, core):
+        part[g] = base[:, g * feat:(g + 1) * feat].astype(BF16).reshape(C, CAP, feat)
+
+    NG = 4 if C % 4 == 0 else 1
+    GB = C // NG
+    mine = c // GB
+
+    def span(g):
+        return pl.ds(g * GB, GB)
+
+    def pair_copy(yy, g, core):
         return send_rows(
-            part.at[2 * yy + core], pair.at[yy], pS.at[yy], pR.at[yy], 0, **at_exp(mate)
+            part.at[2 * yy + core, span(g)], pair.at[yy, span(g)], pS.at[yy, g], pR.at[yy, g], 0,
+            **at_exp(mate),
         )
 
-    def sum_copy(yy, came):
-        return send_rows(tosend.at[yy], fromy.at[came], qS.at[yy], qR.at[came], 0, **at_exp(2 * yy + q))
+    def sum_copy(yy, g, came):
+        return send_rows(
+            tosend.at[yy, span(g)], fromy.at[came, span(g)], qS.at[yy, g], qR.at[came, g], 0,
+            **at_exp(2 * yy + q),
+        )
 
     @pl.loop(1, NY + 1)
     def _(j):
-        pair_copy(lax.rem(y + j, NY), 1 - q).start()
-
-    @pl.loop(1, NY)
+        @pl.loop(1, NG + 1)
+        def _(n):
+            pair_copy(lax.rem(y + j, NY), lax.rem(mine + n, NG), 1 - q).start()
+
+    @pl.loop(1, NG + 1)
+    def _(n):
+        g = lax.rem(mine + n, NG)
+
+        @pl.loop(1, NY)
+        def _(j):
+            yy = lax.rem(y + j, NY)
+            pair_copy(yy, g, q).wait_recv()
+            tosend[yy, span(g)] = (
+                part[2 * yy + q, span(g)].astype(F32) + pair[yy, span(g)].astype(F32)
+            ).astype(BF16)
+            sum_copy(yy, g, y).start()
+
+    @pl.loop(1, F)
     def _(j):
-        yy = lax.rem(y + j, NY)
-        pair_copy(yy, q).wait_recv()
-        tosend[yy] = (part[2 * yy + q].astype(F32) + pair[yy].astype(F32)).astype(BF16)
-        sum_copy(yy, y).start()
+        other = lax.rem(f - j + F, F)
+        rank_copy(rank_l, lS, lR, other, other).wait_recv()
+
+    low = rank_l[0].astype(F32)
+    for g in range(1, F):
+        low = low + rank_l[g].astype(F32)
+    low = low.astype(BF16)
+    adapt[...] = (ADAPTER_SCALE * dot(low, adu[...], TN)).reshape(C, CAP, feat)
+
+    @pl.loop(1, NG + 1)
+    def _(n):
+        g = lax.rem(mine + n, NG)
+        pair_copy(y, g, q).wait_recv()
+        adapt[span(g)] += part[f, span(g)].astype(F32) + pair[y, span(g)].astype(F32)
+
+        @pl.loop(1, NY)
+        def _(j):
+            yy = lax.rem(y - j + NY, NY)
+            sum_copy(y, g, yy).wait_recv()
+            adapt[span(g)] += fromy[yy, span(g)].astype(F32)
+
+        outrows[span(g)] = adapt[span(g)].astype(BF16)
+
+        @pl.loop(0, GB)
+        def _(i):
+            other = g * GB + i
+
+            @pl.when(other != c)
+            def _():
+                ret_copy(other, c).start()
+
+    ret[c] = outrows[c]
+
+    @pl.loop(1, C)
+    def _(i):
+        b = lax.rem(c - i + C, C)
+        grad_copy(b, b).wait_recv()
+
+    grads = gin[...].reshape(R, feat)
+    rank_b[f] = dot(adu[...], grads, NT).astype(BF16)
+
+    @pl.loop(1, F)
+    def _(j):
+        rank_copy(rank_b, bS, bR, lax.rem(f + j, F), f).start()
 
     @pl.loop(1, F)
     def _(j):
         other = lax.rem(f - j + F, F)
         rank_copy(rank_b, bS, bR, other, other).wait_recv()
-        rank_copy(rank_l, lS, lR, other, other).wait_recv()
-
-    low = rank_l[0].astype(F32)
+
     back = rank_b[0].astype(F32)
     for g in range(1, F):
-        low = low + rank_l[g].astype(F32)
         back = back + rank_b[g].astype(F32)
-    low = low.astype(BF16)
     back = (ADAPTER_SCALE * back).astype(BF16)
     lg_v[...] = dot(back, activated, NN)
     rg_v[...] = ADAPTER_SCALE * dot(low, grads, NN)
-    pltpu.make_async_copy(lg_v, lg_h, store.at[0]).start()
-    pltpu.make_async_copy(rg_v, rg_h, store.at[1]).start()
-    adapted = ADAPTER_SCALE * dot(low, right, TN)
-
-    pair_copy(y, q).wait_recv()
-    total = part[f].astype(F32) + pair[y].astype(F32) + adapted
-    base[:, 0:feat] = total
-
-    @pl.loop(1, NY)
-    def _(j):
-        yy = lax.rem(y - j + NY, NY)
-        sum_copy(y, yy).wait_recv()
-        base[:, 0:feat] += fromy[yy].astype(F32)
-
-    outrows[...] = base[:, 0:feat].astype(BF16).reshape(C, CAP, feat)
-
-    @pl.loop(1, C)
-    def _(i):
-        other = lax.rem(c + i, C)
-        ret_copy(other, c).start()
-
-    ret[c] = outrows[c]
 
     @pl.loop(1, C)
     def _(i):
@@ -340,35 +366,43 @@
         rank_copy(rank_b, bS, bR, other, f).wait_send()
         rank_copy(rank_l, lS, lR, other, f).wait_send()
 
-    @pl.loop(0, NY)
-    def _(yy):
-        pair_copy(yy, 1 - q).wait_send()
-
-    @pl.loop(1, NY)
-    def _(j):
-        sum_copy(lax.rem(y + j, NY), y).wait_send()
-
-    wfull = wd[...]
-    whigh = wfull.astype(BF16)
-    wlow = (wfull - whigh.astype(F32)).astype(BF16)
+    @pl.loop(0, NG)
+    def _(g):
+        @pl.loop(0, NY)
+        def _(yy):
+            pair_copy(yy, g, 1 - q).wait_send()
+
+        @pl.loop(1, NY)
+        def _(j):
+            sum_copy(lax.rem(y + j, NY), g, y).wait_send()
 
     @pl.loop(1, C)
     def _(i):
         b = lax.rem(c - i + C, C)
         ret_copy(b, b).wait_recv()
 
-    back_rows = ret[...].reshape(R, feat)
-    out_v[...] = (dot(back_rows, whigh, TN) + dot(back_rows, wlow, TN)).astype(BF16)
-    pltpu.make_async_copy(out_v, out_h, store.at[2]).start()
-
     @pl.loop(1, C)
     def _(i):
         other = lax.rem(c + i, C)
         ret_copy(other, c).wait_send()
 
-    pltpu.make_async_copy(lg_v, lg_h, store.at[0]).wait()
-    pltpu.make_async_copy(rg_v, rg_h, store.at[1]).wait()
-    pltpu.make_async_copy(out_v, out_h, store.at[2]).wait()
+
+def combine_kernel(ret, wd, lg, rg, out_h, lg_h, rg_h, out, sems):
+    C, _, feat = ret.shape
+    left = pltpu.make_async_copy(lg, lg_h, sems.at[0])
+    right = pltpu.make_async_copy(rg, rg_h, sems.at[1])
+    left.start()
+    right.start()
+    weight = wd[...]
+    high = weight.astype(BF16)
+    rest = (weight - high.astype(F32)).astype(BF16)
+    rows = ret[...].reshape(C * CAP, feat)
+    out[...] = (dot(rows, high, TN) + dot(rows, rest, TN)).astype(BF16)
+    result = pltpu.make_async_copy(out, out_h, sems.at[2])
+    result.start()
+    left.wait()
+    right.wait()
+    result.wait()
 
 
 def on_device(
@@ -394,6 +428,7 @@
     NB = width // BLOCK
     hpad = -(-H // 128) * 128
     bpad = -(-NB // 128) * 128
+    NG = 4 if C % 4 == 0 else 1
     dma = pltpu.SemaphoreType.DMA
     scratch = [
         pltpu.VMEM((feat, T), BF16),
@@ -413,51 +448,66 @@
         pltpu.VMEM((F, C, CAP, feat), BF16),
         pltpu.VMEM((C, CAP, feat), BF16),
         pltpu.VMEM((R, width), BF16),
-        pltpu.VMEM((R, T), F32),
         pltpu.VMEM((R, width), F32),
-        pltpu.VMEM((F, R, feat), BF16),
-        pltpu.VMEM((NY, R, feat), BF16),
-        pltpu.VMEM((NY, R, feat), BF16),
-        pltpu.VMEM((NY, R, feat), BF16),
+        pltpu.VMEM((F, C, CAP, feat), BF16),
+        pltpu.VMEM((NY, C, CAP, feat), BF16),
+        pltpu.VMEM((NY, C, CAP, feat), BF16),
+        pltpu.VMEM((NY, C, CAP, feat), BF16),
         pltpu.VMEM((F, rank, R), BF16),
         pltpu.VMEM((F, rank, R), BF16),
         pltpu.VMEM((C, CAP, feat), BF16),
-        pltpu.VMEM((C, CAP, feat), BF16),
-        pltpu.VMEM((feat, T), BF16),
-        pltpu.VMEM((rank, H), F32),
-        pltpu.VMEM((rank, feat), F32),
-        dma((11,)), dma((3,)),
+        pltpu.VMEM((C, CAP, feat), F32),
+        dma((11,)),
         dma((C,)), dma((C,)), dma((C,)), dma((C,)), dma((C,)), dma((C,)),
         dma((NY, C)), dma((NY, C)), dma((NY, C)), dma((NY, C)),
         dma((F,)), dma((F,)), dma((F,)), dma((F,)),
-        dma((NY,)), dma((NY,)), dma((NY,)), dma((NY,)),
+        dma((NY, NG)), dma((NY, NG)), dma((NY, NG)), dma((NY, NG)),
     ]
-    any_space = pl.BlockSpec(memory_space=pl.ANY)
+    in_hbm = pl.BlockSpec(memory_space=pltpu.HBM)
+    in_vmem = pl.BlockSpec(memory_space=pltpu.VMEM)
+    mid = pl.pallas_call(
+        functools.partial(block_kernel, C, F),
+        out_shape=(
+            jax.ShapeDtypeStruct((C, CAP, feat), BF16),
+            jax.ShapeDtypeStruct((R, T), F32),
+            jax.ShapeDtypeStruct((rank, H), F32),
+            jax.ShapeDtypeStruct((rank, feat), F32),
+        ),
+        in_specs=[in_hbm] * 10,
+        out_specs=(in_vmem,) * 4,
+        scratch_shapes=scratch,
+        compiler_params=pltpu.CompilerParams(
+            collective_id=0, has_side_effects=True, vmem_limit_bytes=52 * 2**20
+        ),
+    )(
+        *(
+            pltpu.with_memory_space_constraint(x, pltpu.HBM)
+            for x in (
+                tokens.T,
+                cotangent.T,
+                expert_indices.T,
+                routing_weights.T,
+                gate_up_weight_blocks[0],
+                jnp.transpose(gate_up_block_scales[0], (2, 0, 1)),
+                down_weight_blocks[0],
+                jnp.transpose(down_block_scales, (2, 0, 1)),
+                adapter_down_matrix[0].T,
+                adapter_up_matrix[0],
+            )
+        )
+    )
     out_t, left_t, right = pl.pallas_call(
-        functools.partial(block_kernel, C, F),
+        combine_kernel,
         out_shape=(
             jax.ShapeDtypeStruct((feat, T), BF16),
             jax.ShapeDtypeStruct((rank, H), F32),
             jax.ShapeDtypeStruct((rank, feat), F32),
         ),
-        in_specs=[any_space] * 10,
-        out_specs=(any_space,) * 3,
-        scratch_shapes=scratch,
-        compiler_params=pltpu.CompilerParams(
-            collective_id=0, has_side_effects=True, vmem_limit_bytes=52 * 2**20
-        ),
-    )(
-        tokens.T,
-        cotangent.T,
-        expert_indices.T,
-        routing_weights.T,
-        gate_up_weight_blocks[0],
-        jnp.transpose(gate_up_block_scales[0], (2, 0, 1)),
-        down_weight_blocks[0],
-        jnp.transpose(down_block_scales, (2, 0, 1)),
-        adapter_down_matrix[0].T,
-        adapter_up_matrix[0],
-    )
+        in_specs=[in_vmem] * 4,
+        out_specs=(in_hbm,) * 3,
+        scratch_shapes=[pltpu.VMEM((feat, T), BF16), dma((3,))],
+        compiler_params=pltpu.CompilerParams(vmem_limit_bytes=16 * 2**20),
+    )(*mid)
     return out_t.T, left_t.T[None], right[None]
 
 

time: 45.8 us -> 34.7 us (0.76)
  local copies, waits for them, and re-layouts: 7.75 us -> 0 us
  Pallas kernels: 37 us -> 33.9 us
    unnamed x17 -> x0, local copies, waits for them, and re-layouts: 7.75 us -> none
    pallas_call x1, Pallas kernels: 37 us -> 32.7 us  [on_device(): pl.pallas_call(functools.partial(block_kernel, C, F), out_shape=(jax.Shap...]
    pallas_call x0 -> x1, Pallas kernels: none -> 1.14 us  [on_device(): pl.pallas_call(combine_kernel, out_shape=(jax.ShapeDtypeStruct((feat, T),...]
where the time goes in v2:
time: 34.7 us; the launch traced here: 34.5 us
  Pallas kernels  33.9 us (98%)
  between operations  0.64 us (2%)
    pallas_call x1, Pallas kernels, on_device(): pl.pallas_call(functools.partial(block_kernel, C, F), out_shape=(jax.Shap...  32.7 us
    pallas_call x1, Pallas kernels, on_device(): pl.pallas_call(combine_kernel, out_shape=(jax.ShapeDtypeStruct((feat, T),...  1.14 us

profile of v2, /device:TPU:0, one launch (start us, length us, event | category | flops | bytes accessed | tf_op | source)
XLA Modules:
  0.0 34.5 jit_solution(18138957066233798302)
XLA Ops:
  0.6 32.7 %shard_map.121 = (bf16[8,16,720]{2,1,0:T(8,128)(2,1)S(1)}, f32[128,256]{1,0:T(8,128)S(1)}, f32[16,720]{1,0:T(8,128)S(1)}, f32[16,720]{1,0:T(8,128)S(1)}) custom-call(bf16[720,256]{1,0:T(8,128)(2,1)} %bitcast.22, bf16[720,256]{1,0:T(8,128)(2,1)} %bitcast.23, s32[4,256]{1,0:T(4,128)} %bitcast.27, f32[4,256]{1,0:T(4,128)} %bitcast.28, ...), custom_call_target="tpu_custom_call" | custom-call | tf_op jit(solution)/shard_map/pallas_call | solution.py:468
  33.4 1.1 %shard_map.122 = (bf16[720,256]{1,0:T(8,128)(2,1)}, f32[16,720]{1,0:T(8,128)}, f32[16,720]{1,0:T(8,128)}) custom-call(bf16[8,16,720]{2,1,0:T(8,128)(2,1)S(1)} %get-tuple-element.10.ret, f32[128,256]{1,0:T(8,128)S(1)} %get-tuple-element.11.wd, f32[16,720]{1,0:T(8,128)S(1)} %get-tuple-element.12.lg, f32[16,720]{1,0:T(8,128)S(1)} %get-tuple-element.13.rg), custom_call_target="tpu_custom_call" | custom-call | tf_op jit(solution)/shard_map/pallas_call | solution.py:499

commit v3 on v2

--- a/solution.py
+++ b/solution.py
@@ -25,7 +25,7 @@
 
 
 def unit_rows(hidden):
-    for rows in (240, 144, 128, 80, 48, 16):
+    for rows in (144, 128, 80, 48, 16):
         if hidden % rows == 0:
             return rows
     return hidden
@@ -36,7 +36,7 @@
     tok_h, cot_h, idx_h, rw_h, gu_h, gus_h, dn_h, dns_h, adl_h, adu_h,
     ret, wd, lg_v, rg_v,
     tok, cot, idx, rw, raw, gus, dns, adl, adu,
-    spad, ssc, expand, rows, grows, xin, gin, xfull,
+    spad, ssc, expand, rows, grows, xin, gin, xh, acc,
     base, part, pair, tosend, fromy, rank_b, rank_l, outrows, adapt,
     load, tS, tR, gS, gR, rS, rR, yS, yR, kS, kR, bS, bR, lS, lR, pS, pR, qS, qR,
 ):
@@ -57,6 +57,20 @@
 
     def at_exp(other):
         return dict(device_id=(c, other), device_id_type=pl.DeviceIdType.MESH)
+
+    def paired(me, i, n):
+        if n & (n - 1):
+            return lax.rem(me + i, n)
+        other, bit = 0, 1
+        while bit < n:
+            other = other + lax.rem(me // bit + i // bit, 2) * bit
+            bit *= 2
+        return other
+
+    def from_pair(me, i, n):
+        if n & (n - 1):
+            return lax.rem(me - i + n, n)
+        return paired(me, i, n)
 
     barrier = pltpu.get_barrier_semaphore()
 
@@ -84,6 +98,13 @@
     for copy in loads:
         copy.start()
 
+    expand[...] = (
+        lax.shift_right_logical(lax.broadcasted_iota(jnp.int32, expand.shape, 1), 5)
+        == lax.broadcasted_iota(jnp.int32, expand.shape, 0)
+    ).astype(F32).astype(BF16)
+    spad[...] = jnp.zeros_like(spad)
+    xh[...] = jnp.zeros_like(xh)
+
     loads[0].wait()
     slot = lax.broadcasted_iota(jnp.int32, (R, T), 0)
     expert = lax.shift_right_logical(slot, 4)
@@ -130,26 +151,23 @@
 
     @pl.loop(1, C)
     def _(i):
-        other = lax.rem(c + i, C)
-        tok_copy(other, c).start()
+        tok_copy(paired(c, C - i, C), c).start()
 
     xin[f, c] = rows[c]
 
-    loads[2].wait()
-    weight = jnp.zeros((R, T), F32)
-    for k in range(idx.shape[0]):
-        weight = weight + jnp.where(idx[k:k + 1, :] == expert, rw[k:k + 1, :], 0.0)
-    weight = jnp.where(hit, weight, 0.0)
-    wd[...] = weight
-    loads[3].wait()
-    picked = dot(pick, cot[...], NT) * jnp.sum(weight, axis=1, keepdims=True)
-    grows[...] = picked.astype(BF16).reshape(C, CAP, feat)
-
-    expand[...] = (
-        lax.shift_right_logical(lax.broadcasted_iota(jnp.int32, expand.shape, 1), 5)
-        == lax.broadcasted_iota(jnp.int32, expand.shape, 0)
-    ).astype(F32).astype(BF16)
-    spad[...] = jnp.zeros_like(spad)
+    def forward(i):
+        b = from_pair(c, i, C)
+
+        if not isinstance(i, int):
+            tok_copy(b, b).wait_recv()
+
+        @pl.loop(1, NY)
+        def _(j):
+            y_copy(b, lax.rem(y + j, NY), y).start()
+
+        k_copy(y, b, q).start()
+    forward(0)
+
     loads[4].wait()
     loads[5].wait()
     for m in range(3):
@@ -171,22 +189,9 @@
             spread = dot(scale, expand[:, lo:hi], NN).astype(BF16)
             raw[m, at, lo:hi] = raw[m, at, lo:hi] * spread
 
-    def forward(i):
-        b = lax.rem(c - i + C, C)
-
-        @pl.when(i > 0)
-        def _():
-            tok_copy(b, b).wait_recv()
-
-        @pl.loop(1, NY)
-        def _(j):
-            y_copy(b, lax.rem(y + j, NY), y).start()
-
-        k_copy(y, b, q).start()
-
     def y_forward(i):
         yy = lax.rem(y - 1 - i // C + NY, NY)
-        b = lax.rem(c - lax.rem(i, C) + C, C)
+        b = from_pair(c, lax.rem(i, C), C)
         y_copy(b, y, yy).wait_recv()
         k_copy(yy, b, q).start()
 
@@ -204,7 +209,7 @@
         def _():
             dequant(s)
 
-        @pl.when(s < C)
+        @pl.when(jnp.logical_and(s > 0, s < C))
         def _():
             forward(s)
 
@@ -212,27 +217,61 @@
         def _():
             y_forward(s - C)
 
-    @pl.loop(1, C)
-    def _(i):
-        other = lax.rem(c + i, C)
-        grad_copy(other, c).start()
+    loads[2].wait()
+    weight = jnp.zeros((R, T), F32)
+    for k in range(idx.shape[0]):
+        weight = weight + jnp.where(idx[k:k + 1, :] == expert, rw[k:k + 1, :], 0.0)
+    weight = jnp.where(hit, weight, 0.0)
+    wd[...] = weight
+    loads[3].wait()
+    picked = dot(pick, cot[...], NT) * jnp.sum(weight, axis=1, keepdims=True)
+    grows[...] = picked.astype(BF16).reshape(C, CAP, feat)
+
+    @pl.loop(1, C)
+    def _(i):
+        grad_copy(paired(c, C - i, C), c).start()
 
     gin[c] = grows[c]
 
-    @pl.loop(0, NY)
-    def _(yy):
+    def rank_copy(buf, ss, rs, other, came):
+        return send_rows(buf.at[came], buf.at[came], ss.at[other], rs.at[came], other, **at_exp(other))
+
+    def window(yy):
+        lo = 2 * feat * yy // 128 * 128
+        return lo, min(width, -(-2 * feat * (yy + 1) // 128) * 128)
+
+    def arrived(yy):
         @pl.loop(0, C)
         def _(b):
             k_copy(yy, b, 1 - q).wait_recv()
 
-    def rank_copy(buf, ss, rs, other, came):
-        return send_rows(buf.at[came], buf.at[came], ss.at[other], rs.at[came], other, **at_exp(other))
-
-    for g in range(F):
-        xfull[:, g * feat:(g + 1) * feat] = xin[g].reshape(R, feat)
-    x = xfull[...]
-    gate = jnp.minimum(dot(x, raw[0], NT), CLAMP_LIMIT)
-    up = jnp.clip(dot(x, raw[1], NT), -CLAMP_LIMIT, CLAMP_LIMIT)
+    def project(yy):
+        lo, hi = window(yy)
+        at = 2 * feat * yy - lo
+        for core in range(2):
+            xh[yy, :, at:at + feat] = xin[2 * yy + core].reshape(R, feat)
+            at += feat
+        x = xh[yy, :, 0:hi - lo]
+        return dot(x, raw[0, :, lo:hi], NT), dot(x, raw[1, :, lo:hi], NT)
+
+    arrived(y)
+    for yy in range(NY):
+        @pl.when(y == yy)
+        def _():
+            gate_part, up_part = project(yy)
+            acc[0] = gate_part
+            acc[1] = up_part
+
+    for yy in range(NY):
+        @pl.when(y != yy)
+        def _():
+            arrived(yy)
+            gate_part, up_part = project(yy)
+            acc[0] += gate_part
+            acc[1] += up_part
+
+    gate = jnp.minimum(acc[0], CLAMP_LIMIT)
+    up = jnp.clip(acc[1], -CLAMP_LIMIT, CLAMP_LIMIT)
     activated = ((up + 1.0) * gate / (1.0 + jnp.exp(-GLU_ALPHA * gate))).astype(BF16)
 
     loads[9].wait()
@@ -243,9 +282,13 @@
     def _(j):
         rank_copy(rank_l, lS, lR, lax.rem(f + j, F), f).start()
 
-    base[...] = dot(activated, raw[2], NN)
-    for g in range(F):
-        part[g] = base[:, g * feat:(g + 1) * feat].astype(BF16).reshape(C, CAP, feat)
+    def columns(yy):
+        lo, hi = window(yy)
+        base[:, 0:hi - lo] = dot(activated, raw[2, :, lo:hi], NN)
+        at = 2 * feat * yy - lo
+        for core in range(2):
+            part[2 * yy + core] = base[:, at:at + feat].astype(BF16).reshape(C, CAP, feat)
+            at += feat
 
     NG = 4 if C % 4 == 0 else 1
     GB = C // NG
@@ -266,15 +309,20 @@
             **at_exp(2 * yy + q),
         )
 
-    @pl.loop(1, NY + 1)
-    def _(j):
+    def to_mate(yy):
         @pl.loop(1, NG + 1)
         def _(n):
-            pair_copy(lax.rem(y + j, NY), lax.rem(mine + n, NG), 1 - q).start()
+            pair_copy(yy, paired(mine, NG - n, NG), 1 - q).start()
+
+    for yy in range(NY):
+        @pl.when(y != yy)
+        def _():
+            columns(yy)
+            to_mate(yy)
 
     @pl.loop(1, NG + 1)
     def _(n):
-        g = lax.rem(mine + n, NG)
+        g = paired(mine, NG - n, NG)
 
         @pl.loop(1, NY)
         def _(j):
@@ -285,6 +333,12 @@
             ).astype(BF16)
             sum_copy(yy, g, y).start()
 
+    for yy in range(NY):
+        @pl.when(y == yy)
+        def _():
+            columns(yy)
+            to_mate(yy)
+
     @pl.loop(1, F)
     def _(j):
         other = lax.rem(f - j + F, F)
@@ -298,7 +352,7 @@
 
     @pl.loop(1, NG + 1)
     def _(n):
-        g = lax.rem(mine + n, NG)
+        g = paired(mine, NG - n, NG)
         pair_copy(y, g, q).wait_recv()
         adapt[span(g)] += part[f, span(g)].astype(F32) + pair[y, span(g)].astype(F32)
 
@@ -427,6 +481,7 @@
     R = C * CAP
     NB = width // BLOCK
     hpad = -(-H // 128) * 128
+    wide = min(-(-(2 * feat + 127) // 128) * 128, width)
     bpad = -(-NB // 128) * 128
     NG = 4 if C % 4 == 0 else 1
     dma = pltpu.SemaphoreType.DMA
@@ -447,8 +502,9 @@
         pltpu.VMEM((C, CAP, feat), BF16),
         pltpu.VMEM((F, C, CAP, feat), BF16),
         pltpu.VMEM((C, CAP, feat), BF16),
-        pltpu.VMEM((R, width), BF16),
-        pltpu.VMEM((R, width), F32),
+        pltpu.VMEM((NY, R, wide), BF16),
+        pltpu.VMEM((2, R, H), F32),
+        pltpu.VMEM((R, wide), F32),
         pltpu.VMEM((F, C, CAP, feat), BF16),
         pltpu.VMEM((NY, C, CAP, feat), BF16),
         pltpu.VMEM((NY, C, CAP, feat), BF16),

time: 34.7 us -> 34.4 us (level)
  no operation moved by 1% of the time
where the time goes in v3:
time: 34.4 us; the launch traced here: 34.3 us
  Pallas kernels  33.6 us (98%)
  between operations  0.64 us (2%)
    pallas_call x1, Pallas kernels, on_device(): pl.pallas_call(functools.partial(block_kernel, C, F), out_shape=(jax.Shap...  32.5 us
    pallas_call x1, Pallas kernels, on_device(): pl.pallas_call(combine_kernel, out_shape=(jax.ShapeDtypeStruct((feat, T),...  1.14 us

profile of v3, /device:TPU:0, one launch (start us, length us, event | category | flops | bytes accessed | tf_op | source)
XLA Modules:
  0.0 34.3 jit_solution(528975187252320977)
XLA Ops:
  0.6 32.5 %shard_map.121 = (bf16[8,16,720]{2,1,0:T(8,128)(2,1)S(1)}, f32[128,256]{1,0:T(8,128)S(1)}, f32[16,720]{1,0:T(8,128)S(1)}, f32[16,720]{1,0:T(8,128)S(1)}) custom-call(bf16[720,256]{1,0:T(8,128)(2,1)} %bitcast.22, bf16[720,256]{1,0:T(8,128)(2,1)} %bitcast.23, s32[4,256]{1,0:T(4,128)} %bitcast.27, f32[4,256]{1,0:T(4,128)} %bitcast.28, ...), custom_call_target="tpu_custom_call" | custom-call | tf_op jit(solution)/shard_map/pallas_call | solution.py:524
  33.1 1.1 %shard_map.122 = (bf16[720,256]{1,0:T(8,128)(2,1)}, f32[16,720]{1,0:T(8,128)}, f32[16,720]{1,0:T(8,128)}) custom-call(bf16[8,16,720]{2,1,0:T(8,128)(2,1)S(1)} %get-tuple-element.10.ret, f32[128,256]{1,0:T(8,128)S(1)} %get-tuple-element.11.wd, f32[16,720]{1,0:T(8,128)S(1)} %get-tuple-element.12.lg, f32[16,720]{1,0:T(8,128)S(1)} %get-tuple-element.13.rg), custom_call_target="tpu_custom_call" | custom-call | tf_op jit(solution)/shard_map/pallas_call | solution.py:555

commit v4 on v3

--- a/solution.py
+++ b/solution.py
@@ -36,7 +36,7 @@
     tok_h, cot_h, idx_h, rw_h, gu_h, gus_h, dn_h, dns_h, adl_h, adu_h,
     ret, wd, lg_v, rg_v,
     tok, cot, idx, rw, raw, gus, dns, adl, adu,
-    spad, ssc, expand, rows, grows, xin, gin, xh, acc,
+    spad, ssc, expand, rows, grows, xin, gin, xh, acc, turn,
     base, part, pair, tosend, fromy, rank_b, rank_l, outrows, adapt,
     load, tS, tR, gS, gR, rS, rR, yS, yR, kS, kR, bS, bR, lS, lR, pS, pR, qS, qR,
 ):
@@ -198,8 +198,10 @@
     units = 3 * per
     events = NY * C
 
-    @pl.loop(0, max(events, units))
-    def _(s):
+    def rank_copy(buf, ss, rs, other, came):
+        return send_rows(buf.at[came], buf.at[came], ss.at[other], rs.at[came], other, **at_exp(other))
+
+    def weights_step(s):
         for m in range(3):
             @pl.when(s == m * per)
             def _():
@@ -209,20 +211,20 @@
         def _():
             dequant(s)
 
-        @pl.when(jnp.logical_and(s > 0, s < C))
+    @pl.loop(0, C)
+    def _(s):
+        weights_step(s)
+
+        @pl.when(s > 0)
         def _():
             forward(s)
-
-        @pl.when(jnp.logical_and(s >= C, s < events))
-        def _():
-            y_forward(s - C)
 
     loads[2].wait()
     weight = jnp.zeros((R, T), F32)
     for k in range(idx.shape[0]):
         weight = weight + jnp.where(idx[k:k + 1, :] == expert, rw[k:k + 1, :], 0.0)
     weight = jnp.where(hit, weight, 0.0)
-    wd[...] = weight
+    wd[...] = weight.astype(BF16)
     loads[3].wait()
     picked = dot(pick, cot[...], NT) * jnp.sum(weight, axis=1, keepdims=True)
     grows[...] = picked.astype(BF16).reshape(C, CAP, feat)
@@ -233,8 +235,13 @@
 
     gin[c] = grows[c]
 
-    def rank_copy(buf, ss, rs, other, came):
-        return send_rows(buf.at[came], buf.at[came], ss.at[other], rs.at[came], other, **at_exp(other))
+    @pl.loop(C, max(events, units))
+    def _(s):
+        weights_step(s)
+
+        @pl.when(s < events)
+        def _():
+            y_forward(s - C)
 
     def window(yy):
         lo = 2 * feat * yy // 128 * 128
@@ -252,7 +259,7 @@
             xh[yy, :, at:at + feat] = xin[2 * yy + core].reshape(R, feat)
             at += feat
         x = xh[yy, :, 0:hi - lo]
-        return dot(x, raw[0, :, lo:hi], NT), dot(x, raw[1, :, lo:hi], NT)
+        return dot(raw[0, :, lo:hi], x, NT), dot(raw[1, :, lo:hi], x, NT)
 
     arrived(y)
     for yy in range(NY):
@@ -272,23 +279,15 @@
 
     gate = jnp.minimum(acc[0], CLAMP_LIMIT)
     up = jnp.clip(acc[1], -CLAMP_LIMIT, CLAMP_LIMIT)
-    activated = ((up + 1.0) * gate / (1.0 + jnp.exp(-GLU_ALPHA * gate))).astype(BF16)
-
-    loads[9].wait()
-    loads[10].wait()
-    rank_l[f] = dot(adl[...], activated, NT).astype(BF16)
-
-    @pl.loop(1, F)
-    def _(j):
-        rank_copy(rank_l, lS, lR, lax.rem(f + j, F), f).start()
-
-    def columns(yy):
-        lo, hi = window(yy)
+    turn[0:H] = (up + 1.0) * gate / (1.0 + jnp.exp(-GLU_ALPHA * gate))
+    activated = jnp.transpose(turn[...])[:, 0:H].astype(BF16)
+
+    def columns(g):
+        lo = feat * g // 128 * 128
+        hi = min(width, -(-feat * (g + 1) // 128) * 128)
+        at = feat * g - lo
         base[:, 0:hi - lo] = dot(activated, raw[2, :, lo:hi], NN)
-        at = 2 * feat * yy - lo
-        for core in range(2):
-            part[2 * yy + core] = base[:, at:at + feat].astype(BF16).reshape(C, CAP, feat)
-            at += feat
+        part[g] = base[:, at:at + feat].astype(BF16).reshape(C, CAP, feat)
 
     NG = 4 if C % 4 == 0 else 1
     GB = C // NG
@@ -314,11 +313,16 @@
         def _(n):
             pair_copy(yy, paired(mine, NG - n, NG), 1 - q).start()
 
-    for yy in range(NY):
-        @pl.when(y != yy)
-        def _():
-            columns(yy)
-            to_mate(yy)
+    for g in range(F):
+        @pl.when(jnp.logical_and(y != g // 2, q != g % 2))
+        def _():
+            columns(g)
+            to_mate(g // 2)
+
+    for g in range(F):
+        @pl.when(jnp.logical_and(y != g // 2, q == g % 2))
+        def _():
+            columns(g)
 
     @pl.loop(1, NG + 1)
     def _(n):
@@ -333,11 +337,24 @@
             ).astype(BF16)
             sum_copy(yy, g, y).start()
 
-    for yy in range(NY):
-        @pl.when(y == yy)
-        def _():
-            columns(yy)
-            to_mate(yy)
+    for g in range(F):
+        @pl.when(mate == g)
+        def _():
+            columns(g)
+            to_mate(g // 2)
+
+    for g in range(F):
+        @pl.when(f == g)
+        def _():
+            columns(g)
+
+    loads[9].wait()
+    loads[10].wait()
+    rank_l[f] = dot(adl[...], turn[0:H].astype(BF16), NN).astype(BF16)
+
+    @pl.loop(1, F)
+    def _(j):
+        rank_copy(rank_l, lS, lR, lax.rem(f + j, F), f).start()
 
     @pl.loop(1, F)
     def _(j):
@@ -447,11 +464,8 @@
     right = pltpu.make_async_copy(rg, rg_h, sems.at[1])
     left.start()
     right.start()
-    weight = wd[...]
-    high = weight.astype(BF16)
-    rest = (weight - high.astype(F32)).astype(BF16)
     rows = ret[...].reshape(C * CAP, feat)
-    out[...] = (dot(rows, high, TN) + dot(rows, rest, TN)).astype(BF16)
+    out[...] = dot(rows, wd[...], TN).astype(BF16)
     result = pltpu.make_async_copy(out, out_h, sems.at[2])
     result.start()
     left.wait()
@@ -503,7 +517,8 @@
         pltpu.VMEM((F, C, CAP, feat), BF16),
         pltpu.VMEM((C, CAP, feat), BF16),
         pltpu.VMEM((NY, R, wide), BF16),
-        pltpu.VMEM((2, R, H), F32),
+        pltpu.VMEM((2, H, R), F32),
+        pltpu.VMEM((hpad, R), F32),
         pltpu.VMEM((R, wide), F32),
         pltpu.VMEM((F, C, CAP, feat), BF16),
         pltpu.VMEM((NY, C, CAP, feat), BF16),
@@ -525,7 +540,7 @@
         functools.partial(block_kernel, C, F),
         out_shape=(
             jax.ShapeDtypeStruct((C, CAP, feat), BF16),
-            jax.ShapeDtypeStruct((R, T), F32),
+            jax.ShapeDtypeStruct((R, T), BF16),
             jax.ShapeDtypeStruct((rank, H), F32),
             jax.ShapeDtypeStruct((rank, feat), F32),
         ),

time: 34.4 us -> 37.5 us (1.090)
  Pallas kernels: 33.6 us -> 36.7 us
    pallas_call x1, Pallas kernels: 32.5 us -> 35.6 us  [on_device(): pl.pallas_call(functools.partial(block_kernel, C, F), out_shape=(jax.Shap...]
where the time goes in v4:
time: 37.5 us; the launch traced here: 37.3 us
  Pallas kernels  36.7 us (98%)
  between operations  0.64 us (2%)
    pallas_call x1, Pallas kernels, on_device(): pl.pallas_call(functools.partial(block_kernel, C, F), out_shape=(jax.Shap...  35.6 us
    pallas_call x1, Pallas kernels, on_device(): pl.pallas_call(combine_kernel, out_shape=(jax.ShapeDtypeStruct((feat, T),...  1.05 us

profile of v4, /device:TPU:0, one launch (start us, length us, event | category | flops | bytes accessed | tf_op | source)
XLA Modules:
  0.0 37.3 jit_solution(13451310448031468543)
XLA Ops:
  0.6 35.6 %shard_map.121 = (bf16[8,16,720]{2,1,0:T(8,128)(2,1)S(1)}, bf16[128,256]{1,0:T(8,128)(2,1)S(1)}, f32[16,720]{1,0:T(8,128)S(1)}, f32[16,720]{1,0:T(8,128)S(1)}) custom-call(bf16[720,256]{1,0:T(8,128)(2,1)} %bitcast.22, bf16[720,256]{1,0:T(8,128)(2,1)} %bitcast.23, s32[4,256]{1,0:T(4,128)} %bitcast.27, f32[4,256]{1,0:T(4,128)} %bitcast.28, ...), custom_call_target="tpu_custom_call" | custom-call | tf_op jit(solution)/shard_map/pallas_call | solution.py:539
  36.3 1.1 %shard_map.122 = (bf16[720,256]{1,0:T(8,128)(2,1)}, f32[16,720]{1,0:T(8,128)}, f32[16,720]{1,0:T(8,128)}) custom-call(bf16[8,16,720]{2,1,0:T(8,128)(2,1)S(1)} %get-tuple-element.10.ret, bf16[128,256]{1,0:T(8,128)(2,1)S(1)} %get-tuple-element.11.wd, f32[16,720]{1,0:T(8,128)S(1)} %get-tuple-element.12.lg, f32[16,720]{1,0:T(8,128)S(1)} %get-tuple-element.13.rg), custom_call_target="tpu_custom_call" | custom-call | tf_op jit(solution)/shard_map/pallas_call | solution.py:570

commit v5 on v4

--- a/solution.py
+++ b/solution.py
@@ -36,7 +36,7 @@
     tok_h, cot_h, idx_h, rw_h, gu_h, gus_h, dn_h, dns_h, adl_h, adu_h,
     ret, wd, lg_v, rg_v,
     tok, cot, idx, rw, raw, gus, dns, adl, adu,
-    spad, ssc, expand, rows, grows, xin, gin, xh, acc, turn,
+    spad, ssc, expand, rows, grows, xin, gin, xh, act, turn,
     base, part, pair, tosend, fromy, rank_b, rank_l, outrows, adapt,
     load, tS, tR, gS, gR, rS, rR, yS, yR, kS, kR, bS, bR, lS, lR, pS, pR, qS, qR,
 ):
@@ -103,7 +103,6 @@
         == lax.broadcasted_iota(jnp.int32, expand.shape, 0)
     ).astype(F32).astype(BF16)
     spad[...] = jnp.zeros_like(spad)
-    xh[...] = jnp.zeros_like(xh)
 
     loads[0].wait()
     slot = lax.broadcasted_iota(jnp.int32, (R, T), 0)
@@ -211,83 +210,68 @@
         def _():
             dequant(s)
 
-    @pl.loop(0, C)
+    @pl.loop(0, max(events, units))
     def _(s):
         weights_step(s)
 
-        @pl.when(s > 0)
+        @pl.when(jnp.logical_and(s > 0, s < C))
         def _():
             forward(s)
 
-    loads[2].wait()
-    weight = jnp.zeros((R, T), F32)
-    for k in range(idx.shape[0]):
-        weight = weight + jnp.where(idx[k:k + 1, :] == expert, rw[k:k + 1, :], 0.0)
-    weight = jnp.where(hit, weight, 0.0)
-    wd[...] = weight.astype(BF16)
-    loads[3].wait()
-    picked = dot(pick, cot[...], NT) * jnp.sum(weight, axis=1, keepdims=True)
-    grows[...] = picked.astype(BF16).reshape(C, CAP, feat)
-
-    @pl.loop(1, C)
-    def _(i):
-        grad_copy(paired(c, C - i, C), c).start()
-
-    gin[c] = grows[c]
-
-    @pl.loop(C, max(events, units))
-    def _(s):
-        weights_step(s)
-
-        @pl.when(s < events)
+        @pl.when(s == C)
+        def _():
+            loads[2].wait()
+            weight = jnp.zeros((R, T), F32)
+            for k in range(idx.shape[0]):
+                weight = weight + jnp.where(idx[k:k + 1, :] == expert, rw[k:k + 1, :], 0.0)
+            weight = jnp.where(hit, weight, 0.0)
+            wd[...] = weight.astype(BF16)
+            loads[3].wait()
+            picked = dot(pick, cot[...], NT) * jnp.sum(weight, axis=1, keepdims=True)
+            grows[...] = picked.astype(BF16).reshape(C, CAP, feat)
+
+            @pl.loop(1, C)
+            def _(i):
+                grad_copy(paired(c, C - i, C), c).start()
+
+            gin[c] = grows[c]
+
+        @pl.when(jnp.logical_and(s >= C, s < events))
         def _():
             y_forward(s - C)
 
-    def window(yy):
-        lo = 2 * feat * yy // 128 * 128
-        return lo, min(width, -(-2 * feat * (yy + 1) // 128) * 128)
-
-    def arrived(yy):
+    @pl.loop(0, NY)
+    def _(yy):
         @pl.loop(0, C)
         def _(b):
             k_copy(yy, b, 1 - q).wait_recv()
 
-    def project(yy):
-        lo, hi = window(yy)
-        at = 2 * feat * yy - lo
-        for core in range(2):
-            xh[yy, :, at:at + feat] = xin[2 * yy + core].reshape(R, feat)
-            at += feat
-        x = xh[yy, :, 0:hi - lo]
-        return dot(raw[0, :, lo:hi], x, NT), dot(raw[1, :, lo:hi], x, NT)
-
-    arrived(y)
-    for yy in range(NY):
-        @pl.when(y == yy)
-        def _():
-            gate_part, up_part = project(yy)
-            acc[0] = gate_part
-            acc[1] = up_part
-
-    for yy in range(NY):
-        @pl.when(y != yy)
-        def _():
-            arrived(yy)
-            gate_part, up_part = project(yy)
-            acc[0] += gate_part
-            acc[1] += up_part
-
-    gate = jnp.minimum(acc[0], CLAMP_LIMIT)
-    up = jnp.clip(acc[1], -CLAMP_LIMIT, CLAMP_LIMIT)
-    turn[0:H] = (up + 1.0) * gate / (1.0 + jnp.exp(-GLU_ALPHA * gate))
-    activated = jnp.transpose(turn[...])[:, 0:H].astype(BF16)
-
-    def columns(g):
-        lo = feat * g // 128 * 128
-        hi = min(width, -(-feat * (g + 1) // 128) * 128)
-        at = feat * g - lo
-        base[:, 0:hi - lo] = dot(activated, raw[2, :, lo:hi], NN)
-        part[g] = base[:, at:at + feat].astype(BF16).reshape(C, CAP, feat)
+    for g in range(F):
+        xh[:, g * feat:(g + 1) * feat] = xin[g].reshape(R, feat)
+
+    tall = 240 if H % 240 == 0 else H
+
+    @pl.loop(0, H // tall)
+    def _(i):
+        at = pl.ds(pl.multiple_of(i * tall, tall), tall) if tall < H else slice(None)
+        x = xh[...]
+        gate = jnp.minimum(dot(raw[0, at, :], x, NT), CLAMP_LIMIT)
+        up = jnp.clip(dot(raw[1, at, :], x, NT), -CLAMP_LIMIT, CLAMP_LIMIT)
+        turn[at if tall < H else slice(0, H)] = (up + 1.0) * gate / (1.0 + jnp.exp(-GLU_ALPHA * gate))
+
+    act[...] = jnp.transpose(turn[...])[:, 0:H].astype(BF16)
+    activated = act[...]
+
+    @pl.loop(0, width // lanes)
+    def _(n):
+        at = pl.ds(pl.multiple_of(n * lanes, lanes), lanes)
+        base[:, at] = dot(act[...], raw[2, :, at], NN)
+
+    if width % lanes:
+        last = width // lanes * lanes
+        base[:, last:width] = dot(act[...], raw[2, :, last:width], NN)
+    for g in range(F):
+        part[g] = base[:, g * feat:(g + 1) * feat].astype(BF16).reshape(C, CAP, feat)
 
     NG = 4 if C % 4 == 0 else 1
     GB = C // NG
@@ -313,16 +297,9 @@
         def _(n):
             pair_copy(yy, paired(mine, NG - n, NG), 1 - q).start()
 
-    for g in range(F):
-        @pl.when(jnp.logical_and(y != g // 2, q != g % 2))
-        def _():
-            columns(g)
-            to_mate(g // 2)
-
-    for g in range(F):
-        @pl.when(jnp.logical_and(y != g // 2, q == g % 2))
-        def _():
-            columns(g)
+    @pl.loop(1, NY + 1)
+    def _(j):
+        to_mate(lax.rem(y + j, NY))
 
     @pl.loop(1, NG + 1)
     def _(n):
@@ -336,17 +313,6 @@
                 part[2 * yy + q, span(g)].astype(F32) + pair[yy, span(g)].astype(F32)
             ).astype(BF16)
             sum_copy(yy, g, y).start()
-
-    for g in range(F):
-        @pl.when(mate == g)
-        def _():
-            columns(g)
-            to_mate(g // 2)
-
-    for g in range(F):
-        @pl.when(f == g)
-        def _():
-            columns(g)
 
     loads[9].wait()
     loads[10].wait()
@@ -495,7 +461,6 @@
     R = C * CAP
     NB = width // BLOCK
     hpad = -(-H // 128) * 128
-    wide = min(-(-(2 * feat + 127) // 128) * 128, width)
     bpad = -(-NB // 128) * 128
     NG = 4 if C % 4 == 0 else 1
     dma = pltpu.SemaphoreType.DMA
@@ -516,10 +481,10 @@
         pltpu.VMEM((C, CAP, feat), BF16),
         pltpu.VMEM((F, C, CAP, feat), BF16),
         pltpu.VMEM((C, CAP, feat), BF16),
-        pltpu.VMEM((NY, R, wide), BF16),
-        pltpu.VMEM((2, H, R), F32),
+        pltpu.VMEM((R, width), BF16),
+        pltpu.VMEM((R, H), BF16),
         pltpu.VMEM((hpad, R), F32),
-        pltpu.VMEM((R, wide), F32),
+        pltpu.VMEM((R, width), F32),
         pltpu.VMEM((F, C, CAP, feat), BF16),
         pltpu.VMEM((NY, C, CAP, feat), BF16),
         pltpu.VMEM((NY, C, CAP, feat), BF16),

time: 37.5 us -> 40.7 us (1.085)
  Pallas kernels: 36.7 us -> 39.9 us
    pallas_call x1, Pallas kernels: 35.6 us -> 38.8 us  [on_device(): pl.pallas_call(functools.partial(block_kernel, C, F), out_shape=(jax.Shap...]
where the time goes in v5:
time: 40.7 us; the launch traced here: 40.5 us
  Pallas kernels  39.9 us (98%)
  between operations  0.64 us (2%)
    pallas_call x1, Pallas kernels, on_device(): pl.pallas_call(functools.partial(block_kernel, C, F), out_shape=(jax.Shap...  38.8 us
    pallas_call x1, Pallas kernels, on_device(): pl.pallas_call(combine_kernel, out_shape=(jax.ShapeDtypeStruct((feat, T),...  1.05 us

profile of v5, /device:TPU:0, one launch (start us, length us, event | category | flops | bytes accessed | tf_op | source)
XLA Modules:
  0.0 40.5 jit_solution(2178676790088661395)
XLA Ops:
  0.6 38.8 %shard_map.121 = (bf16[8,16,720]{2,1,0:T(8,128)(2,1)S(1)}, bf16[128,256]{1,0:T(8,128)(2,1)S(1)}, f32[16,720]{1,0:T(8,128)S(1)}, f32[16,720]{1,0:T(8,128)S(1)}) custom-call(bf16[720,256]{1,0:T(8,128)(2,1)} %bitcast.22, bf16[720,256]{1,0:T(8,128)(2,1)} %bitcast.23, s32[4,256]{1,0:T(4,128)} %bitcast.27, f32[4,256]{1,0:T(4,128)} %bitcast.28, ...), custom_call_target="tpu_custom_call" | custom-call | tf_op jit(solution)/shard_map/pallas_call | solution.py:504
  39.5 1.1 %shard_map.122 = (bf16[720,256]{1,0:T(8,128)(2,1)}, f32[16,720]{1,0:T(8,128)}, f32[16,720]{1,0:T(8,128)}) custom-call(bf16[8,16,720]{2,1,0:T(8,128)(2,1)S(1)} %get-tuple-element.10.ret, bf16[128,256]{1,0:T(8,128)(2,1)S(1)} %get-tuple-element.11.wd, f32[16,720]{1,0:T(8,128)S(1)} %get-tuple-element.12.lg, f32[16,720]{1,0:T(8,128)S(1)} %get-tuple-element.13.rg), custom_call_target="tpu_custom_call" | custom-call | tf_op jit(solution)/shard_map/pallas_call | solution.py:535

commit v6 on v3

--- a/solution.py
+++ b/solution.py
@@ -175,7 +175,7 @@
             spad[0:NB, 0:H] = gus[:, m, :]
         else:
             spad[0:NB, 0:H] = dns[:, 0, :]
-        ssc[m] = jnp.transpose(spad[...]).astype(BF16)[0:H]
+        ssc[m] = jnp.transpose(spad[...])[0:H]
     unit = unit_rows(H)
     per = H // unit
     lanes = 256
@@ -184,10 +184,18 @@
         m = u // per
         at = pl.ds(pl.multiple_of(lax.rem(u, per) * unit, unit), unit) if per > 1 else slice(None)
         scale = ssc[m, at, :]
+        narrow = scale.astype(BF16)
+        lane = lax.shift_right_logical(lax.broadcasted_iota(jnp.int32, scale.shape, 1), 5)
         for lo in range(0, width, lanes):
             hi = min(lo + lanes, width)
-            spread = dot(scale, expand[:, lo:hi], NN).astype(BF16)
-            raw[m, at, lo:hi] = raw[m, at, lo:hi] * spread
+            if lo // lanes % 3 == 2 and hi - lo == lanes:
+                for at_lane in range(lo, hi, 128):
+                    here = slice(at_lane, at_lane + 128)
+                    spread = jnp.take_along_axis(scale, lane + at_lane // BLOCK, axis=1).astype(BF16)
+                    raw[m, at, here] = raw[m, at, here] * spread
+            else:
+                spread = dot(narrow, expand[:, lo:hi], NN).astype(BF16)
+                raw[m, at, lo:hi] = raw[m, at, lo:hi] * spread
 
     def y_forward(i):
         yy = lax.rem(y - 1 - i // C + NY, NY)
@@ -213,25 +221,27 @@
         def _():
             forward(s)
 
+        @pl.when(s == C)
+        def _():
+            loads[2].wait()
+            weight = jnp.zeros((R, T), F32)
+            for k in range(idx.shape[0]):
+                weight = weight + jnp.where(idx[k:k + 1, :] == expert, rw[k:k + 1, :], 0.0)
+            weight = jnp.where(hit, weight, 0.0)
+            wd[...] = weight.astype(BF16)
+            loads[3].wait()
+            picked = dot(pick, cot[...], NT) * jnp.sum(weight, axis=1, keepdims=True)
+            grows[...] = picked.astype(BF16).reshape(C, CAP, feat)
+
+            @pl.loop(1, C)
+            def _(i):
+                grad_copy(paired(c, C - i, C), c).start()
+
+            gin[c] = grows[c]
+
         @pl.when(jnp.logical_and(s >= C, s < events))
         def _():
             y_forward(s - C)
-
-    loads[2].wait()
-    weight = jnp.zeros((R, T), F32)
-    for k in range(idx.shape[0]):
-        weight = weight + jnp.where(idx[k:k + 1, :] == expert, rw[k:k + 1, :], 0.0)
-    weight = jnp.where(hit, weight, 0.0)
-    wd[...] = weight
-    loads[3].wait()
-    picked = dot(pick, cot[...], NT) * jnp.sum(weight, axis=1, keepdims=True)
-    grows[...] = picked.astype(BF16).reshape(C, CAP, feat)
-
-    @pl.loop(1, C)
-    def _(i):
-        grad_copy(paired(c, C - i, C), c).start()
-
-    gin[c] = grows[c]
 
     def rank_copy(buf, ss, rs, other, came):
         return send_rows(buf.at[came], buf.at[came], ss.at[other], rs.at[came], other, **at_exp(other))
@@ -447,11 +457,8 @@
     right = pltpu.make_async_copy(rg, rg_h, sems.at[1])
     left.start()
     right.start()
-    weight = wd[...]
-    high = weight.astype(BF16)
-    rest = (weight - high.astype(F32)).astype(BF16)
     rows = ret[...].reshape(C * CAP, feat)
-    out[...] = (dot(rows, high, TN) + dot(rows, rest, TN)).astype(BF16)
+    out[...] = dot(rows, wd[...], TN).astype(BF16)
     result = pltpu.make_async_copy(out, out_h, sems.at[2])
     result.start()
     left.wait()
@@ -496,7 +503,7 @@
         pltpu.VMEM((rank, H), BF16),
         pltpu.VMEM((rank, feat), BF16),
         pltpu.VMEM((bpad, hpad), F32),
-        pltpu.VMEM((3, H, bpad), BF16),
+        pltpu.VMEM((3, H, bpad), F32),
         pltpu.VMEM((bpad, width), BF16),
         pltpu.VMEM((C, CAP, feat), BF16),
         pltpu.VMEM((C, CAP, feat), BF16),
@@ -525,7 +532,7 @@
         functools.partial(block_kernel, C, F),
         out_shape=(
             jax.ShapeDtypeStruct((C, CAP, feat), BF16),
-            jax.ShapeDtypeStruct((R, T), F32),
+            jax.ShapeDtypeStruct((R, T), BF16),
             jax.ShapeDtypeStruct((rank, H), F32),
             jax.ShapeDtypeStruct((rank, feat), F32),
         ),

time: 34.4 us -> 34.2 us (level)
  no operation moved by 1% of the time
where the time goes in v6:
time: 34.2 us; the launch traced here: 34 us
  Pallas kernels  33.4 us (98%)
  between operations  0.64 us (2%)
    pallas_call x1, Pallas kernels, on_device(): pl.pallas_call(functools.partial(block_kernel, C, F), out_shape=(jax.Shap...  32.3 us
    pallas_call x1, Pallas kernels, on_device(): pl.pallas_call(combine_kernel, out_shape=(jax.ShapeDtypeStruct((feat, T),...  1.05 us

profile of v6, /device:TPU:0, one launch (start us, length us, event | category | flops | bytes accessed | tf_op | source)
XLA Modules:
  0.0 34.0 jit_solution(3803692951161027021)
XLA Ops:
  0.6 32.3 %shard_map.121 = (bf16[8,16,720]{2,1,0:T(8,128)(2,1)S(1)}, bf16[128,256]{1,0:T(8,128)(2,1)S(1)}, f32[16,720]{1,0:T(8,128)S(1)}, f32[16,720]{1,0:T(8,128)S(1)}) custom-call(bf16[720,256]{1,0:T(8,128)(2,1)} %bitcast.22, bf16[720,256]{1,0:T(8,128)(2,1)} %bitcast.23, s32[4,256]{1,0:T(4,128)} %bitcast.27, f32[4,256]{1,0:T(4,128)} %bitcast.28, ...), custom_call_target="tpu_custom_call" | custom-call | tf_op jit(solution)/shard_map/pallas_call | solution.py:531
  33.0 1.1 %shard_map.122 = (bf16[720,256]{1,0:T(8,128)(2,1)}, f32[16,720]{1,0:T(8,128)}, f32[16,720]{1,0:T(8,128)}) custom-call(bf16[8,16,720]{2,1,0:T(8,128)(2,1)S(1)} %get-tuple-element.10.ret, bf16[128,256]{1,0:T(8,128)(2,1)S(1)} %get-tuple-element.11.wd, f32[16,720]{1,0:T(8,128)S(1)} %get-tuple-element.12.lg, f32[16,720]{1,0:T(8,128)S(1)} %get-tuple-element.13.rg), custom_call_target="tpu_custom_call" | custom-call | tf_op jit(solution)/shard_map/pallas_call | solution.py:562
